TPU v7x, 32 devices: a whole 2x2x4 slice. The times are simulated.
32 devices in a mesh: scen: 4 (over y, core), tm: 8 (over z, x).
Axes of the slice: x: 2, y: 2, z: 4, core: 2. Of those that a mesh axis runs over, the one named last changes fastest.
Arguments:
- cotangent: float32 [16, 336, 1024], P('scen', 'tm'), may hold values from -6 to 6
- blocks: bfloat16 [8, 6, 128, 128], P('tm'), may hold values from -0.21875 to 0.21875
- zone_links: int32 [8, 6], replicated, may hold values from 0 to 7, as said below
- step_size: float32 [1024], replicated, may hold values from 0.3 to 1
- coupling: bfloat16 [8, 336, 336], P('tm'), may hold values from -0.3125 to 0.3125
- ramp_band: int32 [8], P('tm'), may hold values from 42 to 336, as said below
- candidates: int32 [512], P('scen'), may hold values from 0 to 1023, as said below
Outputs:
- initial_adjoint: float32 [16, 336, 1024], P('scen', 'tm')
- siting_gradient: float32 [336, 512], P('tm', 'scen')
Inputs may be any that keep to these rules, and one draw needn't show every extreme that they name: zone_links[z, 0] = z, and the 6 entries of a row are distinct zones. `ramp_band`: at least one zone has reach 336. `candidates`: the entries of block m of 128 consecutive entries are distinct buses in m * (256) to (m + 1) * 256 - 1.
All inputs are finite; a program needn't handle non-finite values.
Results may differ from a plain program's by a relative error of at most 0.0029.
Values may be sent and summed in bfloat16 or wider, within the bound.
A program may use at most 64 MiB of HBM per device.

v0:
```python
import jax
import jax.numpy as jnp
from jax import lax
from jax.sharding import PartitionSpec as P

SWEEPS = 2


def network_term(scaled, link_blocks, zone_links):
    scen_count, hour_count, buses = scaled.shape
    link_count, zone_count, bus_width = (
        link_blocks.shape[0],
        link_blocks.shape[1],
        link_blocks.shape[3],
    )
    zone_major = jnp.transpose(
        scaled.reshape(scen_count * hour_count, zone_count, bus_width), (1, 0, 2)
    )
    total = jnp.zeros((zone_count, scen_count * hour_count, bus_width), jnp.float32)
    for link in range(link_count):
        picked = jnp.take(zone_major, zone_links[:, link], axis=0)
        total = total + lax.dot_general(
            picked,
            link_blocks[link],
            (((2,), (1,)), ((0,), (0,))),
            preferred_element_type=jnp.float32,
        )
    return jnp.transpose(total, (1, 0, 2)).reshape(scen_count, hour_count, buses)


def temporal_term(moved, masked_turned):
    scen_count, hour_count, owned = moved.shape
    zone_count = masked_turned.shape[0]
    bus_width = owned // zone_count
    rows = []
    for scen in range(scen_count):
        column = moved[scen, :, 0:bus_width]
        pieces = jnp.dot(masked_turned[0], column, preferred_element_type=jnp.float32)
        rows.append(pieces)
    return jnp.stack(rows, axis=0).astype(jnp.bfloat16)


def per_device(cotangent, blocks, zone_links, step_size, coupling, ramp_band, candidates):
    all_blocks = lax.all_gather(blocks, "tm", axis=0, tiled=True)
    link_blocks = jnp.transpose(all_blocks, (1, 0, 2, 3))
    hour_count = coupling.shape[1]
    hour_ids = jnp.arange(hour_count, dtype=jnp.int32)
    spread = jnp.abs(hour_ids[:, None] - hour_ids[None, :])
    masked = jnp.where(
        spread[None, :, :] <= ramp_band[:, None, None], coupling, jnp.zeros_like(coupling)
    )
    masked_turned = jnp.transpose(masked, (0, 2, 1))
    scen_total = cotangent.shape[0] * lax.axis_size("scen")
    adjoint = cotangent
    grad_local = jnp.zeros((cotangent.shape[1], cotangent.shape[2]), jnp.float32)
    for sweep in range(SWEEPS):
        weighted = adjoint * step_size[None, None, :]
        sweep_grad = jnp.sum(weighted, axis=0) * (1.0 / scen_total)
        grad_local = grad_local + sweep_grad
        scaled = weighted.astype(jnp.bfloat16)
        moved = lax.all_to_all(scaled, "tm", split_axis=2, concat_axis=1, tiled=True)
        temporal = lax.all_to_all(
            temporal_term(moved, masked_turned), "tm", split_axis=1, concat_axis=2, tiled=True
        )
        network = network_term(scaled, link_blocks, zone_links)
        adjoint = adjoint - network - temporal.astype(jnp.float32)
    reduced = lax.psum_scatter(grad_local, "scen", scatter_dimension=1, tiled=True)
    width = reduced.shape[1]
    local_cols = candidates - lax.axis_index("scen") * width
    siting_gradient = jnp.take(reduced, local_cols, axis=1)
    return (adjoint, siting_gradient)


def solution(mesh):
    placed = (
        P("scen", "tm", None),
        P("tm", None, None, None),
        P(),
        P(),
        P("tm", None, None),
        P("tm"),
        P("scen"),
    )
    return jax.shard_map(
        per_device,
        mesh=mesh,
        in_specs=placed,
        out_specs=(P("scen", "tm", None), P("tm", "scen")),
        check_vma=False,
    )
```

profile of v0, /device:TPU:0, one launch (start us, length us, event | category | flops | bytes accessed | tf_op | source)
XLA Modules:
  0.0 146.2 jit_solution(10264485500666120326)
XLA Ops:
  7.9 1.5 %fusion.12 = bf16[4,42,1024]{2,1,0:T(8,128)(2,1)S(1)} fusion(f32[4,42,1024]{2,0,1:T(4,128)} %param.9, f32[1024]{0:T(1024)} %param.12), kind=kLoop, calls=%fused_computation.46 | loop fusion | flops 344064 | bytes 1036288 | tf_op jit(solution)/shard_map/convert_element_type | solution.py:60
  10.2 3.1 %reshape.234 = bf16[8,2,10752]{2,1,0:T(2,128)(2,1)} reshape(bf16[1024,4,42]{2,1,0:T(4,128)(2,1)S(1)} %bitcast.130) | data formatting | bytes 688128
  13.2 7.3 %all-to-all-start = ((bf16[8,2,10752]{2,1,0:T(2,128)(2,1)}), bf16[8,2,10752]{2,1,0:T(2,128)(2,1)S(1)}, u32[]{:S(2)}, u32[]{:S(2)}) async-start(bf16[8,2,10752]{2,1,0:T(2,128)(2,1)} %reshape.234), calls=%async_computation | async-start | bytes 688128 | tf_op jit(solution)/shard_map/all_to_all | solution.py:61
  21.6 15.8 %all-to-all-done = bf16[8,2,10752]{2,1,0:T(2,128)(2,1)S(1)} async-done(((bf16[8,2,10752]{2,1,0:T(2,128)(2,1)}), bf16[8,2,10752]{2,1,0:T(2,128)(2,1)S(1)}, u32[]{:S(2)}, u32[]{:S(2)}) %all-to-all-start) | async-done | bytes 344096 | tf_op jit(solution)/shard_map/all_to_all | solution.py:61
  37.3 3.0 %reshape.235 = bf16[1024,4,42]{2,1,0:T(4,128)(2,1)S(1)} reshape(bf16[8,2,10752]{2,1,0:T(2,128)(2,1)S(1)} %all-to-all-done) | data formatting | bytes 688128
  43.7 3.5 %all-to-all-start.1 = ((bf16[4,336,128]{2,0,1:T(4,128)(2,1)}), bf16[4,336,128]{2,0,1:T(4,128)(2,1)S(1)}, u32[]{:S(2)}, u32[]{:S(2)}) async-start(bf16[4,336,128]{2,0,1:T(4,128)(2,1)} %copy.93), calls=%async_computation.1 | async-start | bytes 688128 | tf_op jit(solution)/shard_map/all_to_all | solution.py:62
  47.7 1.3 gather_fusion.1
  49.0 1.3 gather_fusion.2
  50.4 1.3 gather_fusion.3
  51.7 1.3 gather_fusion.4
  55.0 9.9 %all-to-all-done.1 = bf16[4,336,128]{2,0,1:T(4,128)(2,1)S(1)} async-done(((bf16[4,336,128]{2,0,1:T(4,128)(2,1)}), bf16[4,336,128]{2,0,1:T(4,128)(2,1)S(1)}, u32[]{:S(2)}, u32[]{:S(2)}) %all-to-all-start.1) | async-done | bytes 344096 | tf_op jit(solution)/shard_map/all_to_all | solution.py:62
  66.0 1.6 %fusion.26 = f32[8,168,128]{2,1,0:T(8,128)S(1)} fusion(bf16[8,168,128]{2,1,0:T(8,128)(2,1)} %gather_fusion.1, pred[8]{0:T(512)(128)(4,1)S(1)} %get-tuple-element.43, bf16[6,8,128,128]{3,2,1,0:T(8,128)(2,1)} %bitcast.115), kind=kOutput, calls=%fused_computation.69 | convolution fusion | flops 44212224 | bytes 1294344 | tf_op jit(solution)/shard_map/dot_general | solution.py:22
  67.6 1.5 %convolution_add_fusion.9 = f32[8,168,128]{2,1,0:T(8,128)S(1)} fusion(f32[8,168,128]{2,1,0:T(8,128)S(1)} %fusion.26, bf16[8,168,128]{2,1,0:T(8,128)(2,1)} %gather_fusion.2, pred[8]{0:T(512)(128)(4,1)S(1)} %get-tuple-element.42, bf16[6,8,128,128]{3,2,1,0:T(8,128)(2,1)} %bitcast.116), kind=kOutput, calls=%fused_computation.24 | convolution fusion | flops 44384256 | bytes 1982472 | tf_op jit(solution)/shard_map/dot_general | solution.py:22
  72.1 2.6 %multiply_reduce_fusion = (f32[42,1024]{1,0:T(8,128)}, f32[42,1024]{1,0:T(8,128)}, f32[4,42,1024]{2,1,0:T(8,128)S(1)}) fusion(f32[1024]{0:T(1024)S(1)} %copy-done.10, f32[4,42,1024]{2,0,1:T(4,128)} %param.9, f32[4,42,1024]{2,1,0:T(8,128)S(1)} %reshape.226, f32[4,42,1024]{2,1,0:T(8,128)} %reshape.78), kind=kLoop, calls=%fused_computation.47 | loop fusion | flops 946176 | bytes 3100672 | tf_op jit(solution)/shard_map/reduce_sum | solution.py:58
  75.0 1.3 gather_fusion.7
  77.6 1.3 gather_fusion.10
  79.0 1.3 gather_fusion.11
  80.3 1.5 copy.98
  82.5 1.4 fusion.19
  83.9 4.1 %reshape.236 = bf16[8,2,10752]{2,1,0:T(2,128)(2,1)} reshape(bf16[1024,4,42]{2,1,0:T(4,128)(2,1)} %bitcast.127) | data formatting | bytes 688128
  88.0 4.3 %all-to-all-start.2 = ((bf16[8,2,10752]{2,1,0:T(2,128)(2,1)}), bf16[8,2,10752]{2,1,0:T(2,128)(2,1)}, u32[]{:S(2)}, u32[]{:S(2)}) async-start(bf16[8,2,10752]{2,1,0:T(2,128)(2,1)} %reshape.236), calls=%async_computation.2 | async-start | bytes 688128 | tf_op jit(solution)/shard_map/all_to_all | solution.py:61
  92.3 2.2 %convolution_add_fusion.4 = f32[8,168,128]{2,1,0:T(8,128)} fusion(f32[8,168,128]{2,1,0:T(8,128)S(1)} %fusion.19, bf16[8,168,128]{2,1,0:T(8,128)(2,1)} %gather_fusion.8, pred[8]{0:T(512)(128)(4,1)S(1)} %get-tuple-element.42, bf16[6,8,128,128]{3,2,1,0:T(8,128)(2,1)S(1)} %bitcast.122), kind=kOutput, calls=%fused_computation.18 | convolution fusion | flops 44384256 | bytes 1982976 | tf_op jit(solution)/shard_map/dot_general | solution.py:22
  95.1 1.5 %convolution_add_fusion.3 = f32[8,168,128]{2,1,0:T(8,128)S(1)} fusion(f32[8,168,128]{2,1,0:T(8,128)} %convolution_add_fusion.4, bf16[8,168,128]{2,1,0:T(8,128)(2,1)S(1)} %gather_fusion.9, pred[8]{0:T(512)(128)(4,1)S(1)} %get-tuple-element.41, bf16[6,8,128,128]{3,2,1,0:T(8,128)(2,1)S(1)} %bitcast.123), kind=kOutput, calls=%fused_computation.17 | convolution fusion | flops 44384256 | bytes 1982976 | tf_op jit(solution)/shard_map/dot_general | solution.py:22
  97.1 5.9 %all-to-all-done.2 = bf16[8,2,10752]{2,1,0:T(2,128)(2,1)} async-done(((bf16[8,2,10752]{2,1,0:T(2,128)(2,1)}), bf16[8,2,10752]{2,1,0:T(2,128)(2,1)}, u32[]{:S(2)}, u32[]{:S(2)}) %all-to-all-start.2) | async-done | bytes 344096 | tf_op jit(solution)/shard_map/all_to_all | solution.py:61
  102.9 5.0 %reshape.237 = bf16[1024,4,42]{2,1,0:T(4,128)(2,1)} reshape(bf16[8,2,10752]{2,1,0:T(2,128)(2,1)} %all-to-all-done.2) | data formatting | bytes 688128
  108.0 2.8 %copy.112 = bf16[4,42,8,128]{3,2,0,1:T(8,128)(2,1)} copy(bf16[4,42,8,128]{1,0,3,2:T(4,128)(2,1)} %bitcast.129) | data formatting | bytes 688128 | tf_op jit(solution)/shard_map/all_to_all | solution.py:61
  110.8 1.7 %fusion.74 = (bf16[1,8,42,128]{3,1,0,2:T(8,128)(2,1)S(1)}, bf16[1,8,42,128]{3,1,0,2:T(8,128)(2,1)}, bf16[1,8,42,128]{3,1,0,2:T(8,128)(2,1)}, bf16[1,8,42,128]{3,1,0,2:T(8,128)(2,1)}) fusion(bf16[4,8,42,128]{3,1,0,2:T(8,128)(2,1)} %bitcast.133), kind=kLoop, calls=%fused_computation.143 | loop fusion | bytes 688128 | tf_op jit(solution)/shard_map/slice | solution.py:37
  118.0 1.4 fusion.6
  122.2 4.1 %all-to-all-start.3 = ((bf16[4,336,128]{2,0,1:T(4,128)(2,1)}), bf16[4,336,128]{2,0,1:T(4,128)(2,1)}, u32[]{:S(2)}, u32[]{:S(2)}) async-start(bf16[4,336,128]{2,0,1:T(4,128)(2,1)} %copy.104), calls=%async_computation.3 | async-start | bytes 688128 | tf_op jit(solution)/shard_map/all_to_all | solution.py:62
  126.3 2.2 %convolution_add_fusion.1 = f32[8,168,128]{2,1,0:T(8,128)} fusion(f32[8,168,128]{2,1,0:T(8,128)S(1)} %convolution_add_fusion.2, bf16[8,168,128]{2,1,0:T(8,128)(2,1)} %gather_fusion.11, pred[8]{0:T(512)(128)(4,1)S(1)} %get-tuple-element.39, bf16[6,8,128,128]{3,2,1,0:T(8,128)(2,1)S(1)} %bitcast.125), kind=kOutput, calls=%fused_computation.15 | convolution fusion | flops 44384256 | bytes 1982976 | tf_op jit(solution)/shard_map/dot_general | solution.py:22
  129.1 1.5 %fusion = f32[168,8,128]{2,0,1:T(8,128)S(1)} fusion(f32[8,168,128]{2,1,0:T(8,128)} %convolution_add_fusion.1, bf16[8,168,128]{2,1,0:T(8,128)(2,1)S(1)} %gather_fusion.12, pred[8]{0:T(512)(128)(4,1)S(1)} %get-tuple-element.38, bf16[6,8,128,128]{3,2,1,0:T(8,128)(2,1)S(1)} %bitcast.126), kind=kOutput, calls=%fused_computation.14 | convolution fusion | flops 44384256 | bytes 1982976 | tf_op jit(solution)/shard_map/dot_general | solution.py:22
  133.2 3.4 %all-to-all-done.3 = bf16[4,336,128]{2,0,1:T(4,128)(2,1)} async-done(((bf16[4,336,128]{2,0,1:T(4,128)(2,1)}), bf16[4,336,128]{2,0,1:T(4,128)(2,1)}, u32[]{:S(2)}, u32[]{:S(2)}) %all-to-all-start.3) | async-done | bytes 344096 | tf_op jit(solution)/shard_map/all_to_all | solution.py:62
  (111 shorter events, 28.9 us)
Async XLA Ops:
  7.2 58.9 %all-gather.2.cloned.1.call-start = ((), (), s32[]{:S(2)}) async-start(), calls=%async_computation.5 | async-start | bytes 1769472 | tf_op jit(solution)/shard_map/all_gather | solution.py:44
  9.4 11.1 %copy-start.7 = (s32[8,6]{1,0:T(8,128)S(1)}, s32[8,6]{1,0:T(8,128)}, u32[]{:S(2)}) copy-start(s32[8,6]{1,0:T(8,128)} %param.11) | copy-start | bytes 580
  9.4 12.1 %copy-start.11 = (s32[128]{0:T(128)S(1)}, s32[128]{0:T(128)}, u32[]{:S(2)}) copy-start(s32[128]{0:T(128)} %param.15) | copy-start | bytes 1540
  13.2 24.1 %all-to-all-start = ((bf16[8,2,10752]{2,1,0:T(2,128)(2,1)}), bf16[8,2,10752]{2,1,0:T(2,128)(2,1)S(1)}, u32[]{:S(2)}, u32[]{:S(2)}) async-start(bf16[8,2,10752]{2,1,0:T(2,128)(2,1)} %reshape.234), calls=%async_computation | async-start | bytes 688128 | tf_op jit(solution)/shard_map/all_to_all | solution.py:61
  40.4 1.2 copy-start.12
  43.7 21.3 %all-to-all-start.1 = ((bf16[4,336,128]{2,0,1:T(4,128)(2,1)}), bf16[4,336,128]{2,0,1:T(4,128)(2,1)S(1)}, u32[]{:S(2)}, u32[]{:S(2)}) async-start(bf16[4,336,128]{2,0,1:T(4,128)(2,1)} %copy.93), calls=%async_computation.1 | async-start | bytes 688128 | tf_op jit(solution)/shard_map/all_to_all | solution.py:62
  47.2 83.7 %reduce-scatter.2.cloned.1.call-start = ((), (), s32[]{:S(2)}) async-start(), calls=%async_computation.6 | async-start | bytes 245760 | tf_op jit(solution)/shard_map/reduce_scatter | solution.py:67
  66.0 3.1 %copy-start = (bf16[8,6,128,128]{3,2,0,1:T(8,128)(2,1)S(1)}, bf16[8,6,128,128]{3,2,0,1:T(8,128)(2,1)}, u32[]{:S(2)}) copy-start(bf16[8,6,128,128]{3,2,0,1:T(8,128)(2,1)} %all-gather.2.cloned.1.call-done) | copy-start | bytes 4718596
  66.0 3.1 %copy-start.4 = (bf16[8,168,128]{2,1,0:T(8,128)(2,1)S(1)}, bf16[8,168,128]{2,1,0:T(8,128)(2,1)}, u32[]{:S(2)}) copy-start(bf16[8,168,128]{2,1,0:T(8,128)(2,1)} %gather_fusion.3) | copy-start | bytes 1032196
  67.6 1.9 %copy-start.2 = (bf16[8,168,128]{2,1,0:T(8,128)(2,1)S(1)}, bf16[8,168,128]{2,1,0:T(8,128)(2,1)}, u32[]{:S(2)}) copy-start(bf16[8,168,128]{2,1,0:T(8,128)(2,1)} %gather_fusion.4) | copy-start | bytes 1032196
  69.1 1.0 copy-start.1
  70.9 1.1 copy-start.10
  77.6 4.1 %copy-start.5 = (f32[42,1024]{1,0:T(8,128)S(1)}, f32[42,1024]{1,0:T(8,128)}, u32[]{:S(2)}) copy-start(f32[42,1024]{1,0:T(8,128)} %get-tuple-element.13) | copy-start | bytes 516100
  77.6 4.1 %copy-start.6 = (f32[42,1024]{1,0:T(8,128)S(1)}, f32[42,1024]{1,0:T(8,128)}, u32[]{:S(2)}) copy-start(f32[42,1024]{1,0:T(8,128)} %get-tuple-element.14) | copy-start | bytes 516100
  88.0 15.0 %all-to-all-start.2 = ((bf16[8,2,10752]{2,1,0:T(2,128)(2,1)}), bf16[8,2,10752]{2,1,0:T(2,128)(2,1)}, u32[]{:S(2)}, u32[]{:S(2)}) async-start(bf16[8,2,10752]{2,1,0:T(2,128)(2,1)} %reshape.236), calls=%async_computation.2 | async-start | bytes 688128 | tf_op jit(solution)/shard_map/all_to_all | solution.py:61
  95.1 1.6 %copy-start.3 = (bf16[8,168,128]{2,1,0:T(8,128)(2,1)S(1)}, bf16[8,168,128]{2,1,0:T(8,128)(2,1)}, u32[]{:S(2)}) copy-start(bf16[8,168,128]{2,1,0:T(8,128)(2,1)} %gather_fusion.10) | copy-start | bytes 1032196
  118.0 2.7 %copy-start.8 = (bf16[336,128]{1,0:T(8,128)(2,1)S(1)}, bf16[336,128]{1,0:T(8,128)(2,1)}, u32[]{:S(2)}) copy-start(bf16[336,128]{1,0:T(8,128)(2,1)} %squeeze.101) | copy-start | bytes 258052
  118.0 2.7 %copy-start.13 = (bf16[1,336,336]{2,1,0:T(8,128)(2,1)S(1)}, bf16[1,336,336]{2,1,0:T(8,128)(2,1)}, u32[]{:S(2)}) copy-start(bf16[1,336,336]{2,1,0:T(8,128)(2,1)} %param.13) | copy-start | bytes 677380
  118.0 3.0 %copy-start.9 = (bf16[336,128]{1,0:T(8,128)(2,1)S(1)}, bf16[336,128]{1,0:T(8,128)(2,1)}, u32[]{:S(2)}) copy-start(bf16[336,128]{1,0:T(8,128)(2,1)} %squeeze.102) | copy-start | bytes 258052
  122.2 14.4 %all-to-all-start.3 = ((bf16[4,336,128]{2,0,1:T(4,128)(2,1)}), bf16[4,336,128]{2,0,1:T(4,128)(2,1)}, u32[]{:S(2)}, u32[]{:S(2)}) async-start(bf16[4,336,128]{2,0,1:T(4,128)(2,1)} %copy.104), calls=%async_computation.3 | async-start | bytes 688128 | tf_op jit(solution)/shard_map/all_to_all | solution.py:62
Sparse Core Ops, SparseCore 0:
  10.2 55.8 all-gather.1
  82.6 18.4 reduce-scatter.1
where the time goes:
time: 147 us; the launch traced here: 146 us
  local copies, waits for them, and re-layouts  50.3 us (34%)
  waiting for transfers between devices  36.5 us (25%)
  starting transfers between devices  19.4 us (13%)
  matrix products  18.2 us (12%)
  between operations  15.3 us (10%)
  other arithmetic  6.44 us (4%)
    all_to_all x2, waiting for transfers between devices, per_device(): lax.all_to_all(scaled, 'tm', split_axis=2, concat_axis=1, tiled=True)  21.7 us
    unnamed x34, local copies, waits for them, and re-layouts  17.4 us
    dot_general x12, matrix products, network_term(): lax.dot_general(picked, link_blocks[link], (((2,), (1,)), ((0,), (0,))),...  13.8 us
    gather x12, local copies, waits for them, and re-layouts, network_term(): picked = jnp.take(zone_major, zone_links[:, link], axis=0)  13.8 us
    all_to_all x2, waiting for transfers between devices, per_device(): lax.all_to_all(temporal_term(moved, masked_turned), 'tm', split_axis=1, c...  13.4 us
    all_to_all x2, starting transfers between devices, per_device(): lax.all_to_all(scaled, 'tm', split_axis=2, concat_axis=1, tiled=True)  11.5 us
    all_to_all x2, starting transfers between devices, per_device(): lax.all_to_all(temporal_term(moved, masked_turned), 'tm', split_axis=1, c...  7.59 us
    slice x10, local copies, waits for them, and re-layouts, temporal_term(): column = moved[scen, :, 0:bus_width]  4.6 us
  transfers between devices with their start and end apart: 6, of which 5 were waited for; matrix products, arithmetic and copies ran while one was open for 38% of the time, Pallas kernels for 0%

commit v1 on v0

v1 whole, which is shorter than its diff:
```python
import functools

import jax
import jax.numpy as jnp
from jax import lax
from jax.experimental import pallas as pl
from jax.experimental.pallas import tpu as pltpu
from jax.sharding import PartitionSpec as P

SWEEPS = 2
MESH = pl.DeviceIdType.MESH
F32 = jnp.float32
BF16 = jnp.bfloat16


def padded_coupling(coupling, band, slots, hours, padded):
    total = slots * hours
    rows = lax.broadcasted_iota(jnp.int32, (total, total), 0)
    cols = lax.broadcasted_iota(jnp.int32, (total, total), 1)
    masked = jnp.where(jnp.abs(rows - cols) <= band, coupling.astype(F32), 0.0).astype(BF16)
    wide = lax.broadcasted_iota(jnp.int32, (slots * padded, 1), 0)
    slot = jnp.zeros_like(wide)
    for j in range(1, slots):
        slot = slot + (wide >= j * padded).astype(jnp.int32)
    within = wide - slot * padded
    hour = jnp.where(within < hours, slot * hours + within, -1)
    place = lax.broadcasted_iota(jnp.int32, (slots * padded, total), 1)
    pick = jnp.where(hour == place, 1.0, 0.0).astype(BF16)
    both_last = (((1,), (1,)), ((), ()))
    turned = lax.dot_general(pick, masked, both_last, preferred_element_type=F32).astype(BF16)
    return lax.dot_general(turned, pick, both_last, preferred_element_type=F32).astype(BF16)


def kernel(
    tms, scs,
    cot_ref, blk_ref, links_ref, step_ref, coup_ref, band_ref, cand_ref,
    out_ref, sit_ref,
    adj, sbuf, recv, tsend, trecv, wall, turned, gacc, grecv,
    s_send, s_recv, t_send, t_recv, w1_send, w1_recv, w2_send, w2_recv, w3_send, w3_recv,
    g_send, g_recv,
):
    me = lax.axis_index("tm")
    mine = lax.axis_index("scen")
    scens, hours, _ = cot_ref.shape
    zones, _, padded, bus = adj.shape
    parts = wall.shape[0]
    fan = links_ref.shape[1]
    share = zones // scs

    barrier = pltpu.get_barrier_semaphore()
    for o in range(1, tms):
        pl.semaphore_signal(barrier, inc=1, device_id={"tm": lax.rem(me + o, tms)}, device_id_type=MESH)
    for o in range(1, scs):
        pl.semaphore_signal(barrier, inc=1, device_id={"scen": lax.rem(mine + o, scs)}, device_id_type=MESH)

    def to_tm(src, dst, send, got, o):
        return pltpu.make_async_remote_copy(
            src_ref=src, dst_ref=dst, send_sem=send, recv_sem=got,
            device_id={"tm": lax.rem(me + o, tms)}, device_id_type=MESH,
        )

    def to_scen(src, dst, send, got, peer):
        return pltpu.make_async_remote_copy(
            src_ref=src, dst_ref=dst, send_sem=send, recv_sem=got,
            device_id={"scen": peer}, device_id_type=MESH,
        )

    def scale(sweep, z):
        weighted = adj[z] * step_ref[z][None]
        sbuf[sweep, z] = weighted.astype(BF16)
        part = jnp.sum(weighted, axis=0) * (1.0 / (scens * scs))
        gacc[z] = part if sweep == 0 else gacc[z] + part

    def send_scaled(sweep, o):
        copy = to_tm(
            sbuf.at[sweep, lax.rem(me + o, tms)], recv.at[sweep, me],
            s_send.at[sweep, o], s_recv.at[sweep, o], o,
        )
        copy.start()
        return copy

    def temporal(sweep):
        side = jnp.concatenate(
            [recv[sweep, :, s].reshape(tms * padded, bus) for s in range(scens)], axis=1
        )
        for j in range(tms):
            rows = turned[j * padded:(j + 1) * padded, :]
            term = jnp.dot(rows, side, preferred_element_type=F32).astype(BF16)
            for s in range(scens):
                tsend[sweep, j, s] = term[:, s * bus:(s + 1) * bus]
        copies = []
        for o in range(1, tms):
            copy = to_tm(
                tsend.at[sweep, lax.rem(me + o, tms)], trecv.at[sweep, me],
                t_send.at[sweep, o], t_recv.at[sweep, o], o,
            )
            copy.start()
            copies.append(copy)
        trecv[sweep, me] = tsend[sweep, me]
        return copies

    def network(sweep):
        def one(z, _):
            picked = jnp.concatenate(
                [sbuf[sweep, links_ref[z, k]].reshape(scens * padded, bus) for k in range(fan)], axis=1
            )
            weights = jnp.concatenate([wall[p, z] for p in range(parts)], axis=0)
            term = jnp.dot(picked, weights, preferred_element_type=F32)
            adj[z] = adj[z] - term.reshape(scens, padded, bus)
            return 0

        lax.fori_loop(0, zones, one, 0)

    adj[...] = jnp.zeros_like(adj)
    for s in range(scens):
        for z in range(zones):
            adj[z, s, 0:hours, :] = cot_ref[s, :, z * bus:(z + 1) * bus]

    def first(z, _):
        scale(0, z)
        return 0

    lax.fori_loop(0, zones, first, 0)
    wall[mine, me] = blk_ref[mine]
    pl.semaphore_wait(barrier, tms - 1 + scs - 1)

    sent = []
    scaled_out = [send_scaled(0, o) for o in range(1, tms)]
    recv[0, me] = sbuf[0, me]
    first_leg = []
    for o in range(1, tms):
        copy = to_tm(wall.at[mine, me], wall.at[mine, me], w1_send.at[o], w1_recv.at[o], o)
        copy.start()
        first_leg.append(copy)
    turned[...] = padded_coupling(coup_ref[...], band_ref[0], tms, hours, padded)

    for copy in scaled_out:
        copy.wait_recv()
    temporal_out = temporal(0)
    sent += scaled_out + temporal_out

    for copy in first_leg:
        copy.wait_recv()
    core = lax.rem(mine, 2)
    other = mine + 1 - 2 * core
    second_leg = []
    third_leg = []
    for o in range(1, scs // 2):
        copy = to_scen(
            wall.at[mine], wall.at[mine], w2_send.at[o], w2_recv.at[o], lax.rem(mine + 2 * o, scs)
        )
        copy.start()
        second_leg.append(copy)
    for o in range(scs // 2):
        if o > 0:
            second_leg[o - 1].wait_recv()
        part = lax.rem(mine + scs - 2 * o, scs)
        copy = to_scen(wall.at[part], wall.at[part], w3_send.at[o], w3_recv.at[o], other)
        copy.start()
        third_leg.append(copy)
    for copy in third_leg:
        copy.wait_recv()
    sent += first_leg + second_leg + third_leg

    network(0)
    scaled_out = []
    for o in range(tms):
        zone = lax.rem(me + o, tms)
        if o > 0:
            temporal_out[tms - o - 1].wait_recv()
        adj[zone] = adj[zone] - trecv[0, zone].astype(F32)
        scale(1, zone)
        if o > 0:
            scaled_out.append(send_scaled(1, o))
    recv[1, me] = sbuf[1, me]

    grads = []
    for o in range(1, scs):
        peer = lax.rem(mine + o, scs)
        copy = to_scen(gacc.at[pl.ds(peer * share, share)], grecv.at[o], g_send.at[o], g_recv.at[o], peer)
        copy.start()
        grads.append(copy)

    network(1)
    for copy in scaled_out:
        copy.wait_recv()
    temporal_out = temporal(1)
    sent += scaled_out + temporal_out + grads

    for copy in grads:
        copy.wait_recv()
    total = gacc[pl.ds(mine * share, share)]
    for o in range(1, scs):
        total = total + grecv[o]
    local = cand_ref[...] - mine * (share * bus)
    siting = jnp.zeros((padded, cand_ref.shape[1]), F32)
    for part in range(share):
        ids = lax.broadcasted_iota(jnp.int32, (bus, cand_ref.shape[1]), 0) + part * bus
        chosen = jnp.where(ids == local, 1.0, 0.0)
        siting = siting + jnp.dot(
            total[part], chosen, preferred_element_type=F32, precision=lax.Precision.HIGHEST
        )
    sit_ref[...] = siting[0:hours]

    for copy in temporal_out:
        copy.wait_recv()
    for z in range(zones):
        for s in range(scens):
            value = adj[z, s] - trecv[1, z, s].astype(F32)
            out_ref[s, :, z * bus:(z + 1) * bus] = value[0:hours]
    for copy in sent:
        copy.wait_send()


def per_device(tms, scs, cotangent, blocks, zone_links, step_size, coupling, ramp_band, candidates):
    scens, hours, buses = cotangent.shape
    _, fan, bus, _ = blocks.shape
    zones = buses // bus
    padded = -(-hours // 16) * 16
    rows = fan * bus // scs
    vmem = pl.BlockSpec(memory_space=pltpu.VMEM)
    smem = pl.BlockSpec(memory_space=pltpu.SMEM)
    dma = pltpu.SemaphoreType.DMA
    return pl.pallas_call(
        functools.partial(kernel, tms, scs),
        out_shape=(
            jax.ShapeDtypeStruct(cotangent.shape, F32),
            jax.ShapeDtypeStruct((hours, candidates.shape[0]), F32),
        ),
        in_specs=[vmem, vmem, smem, vmem, vmem, smem, vmem],
        out_specs=(vmem, vmem),
        scratch_shapes=[
            pltpu.VMEM((zones, scens, padded, bus), F32),
            pltpu.VMEM((SWEEPS, zones, scens, padded, bus), BF16),
            pltpu.VMEM((SWEEPS, tms, scens, padded, bus), BF16),
            pltpu.VMEM((SWEEPS, tms, scens, padded, bus), BF16),
            pltpu.VMEM((SWEEPS, zones, scens, padded, bus), BF16),
            pltpu.VMEM((scs, zones, rows, bus), BF16),
            pltpu.VMEM((tms * padded, tms * padded), BF16),
            pltpu.VMEM((zones, padded, bus), F32),
            pltpu.VMEM((scs, zones // scs, padded, bus), F32),
            dma((SWEEPS, tms)), dma((SWEEPS, tms)), dma((SWEEPS, tms)), dma((SWEEPS, tms)),
            dma((tms,)), dma((tms,)), dma((scs,)), dma((scs,)), dma((scs,)), dma((scs,)),
            dma((scs,)), dma((scs,)),
        ],
        compiler_params=pltpu.CompilerParams(
            collective_id=0, has_side_effects=True, vmem_limit_bytes=40 * 1024 * 1024
        ),
        name="sweeps",
    )(
        cotangent,
        blocks.reshape(scs, rows, bus),
        zone_links,
        step_size.reshape(zones, 1, bus),
        coupling.reshape(coupling.shape[1:]),
        ramp_band,
        candidates.reshape(1, -1),
    )


def solution(mesh):
    placed = (
        P("scen", "tm", None),
        P("tm", None, None, None),
        P(),
        P(),
        P("tm", None, None),
        P("tm"),
        P("scen"),
    )
    return jax.shard_map(
        functools.partial(per_device, mesh.shape["tm"], mesh.shape["scen"]),
        mesh=mesh,
        in_specs=placed,
        out_specs=(P("scen", "tm", None), P("tm", "scen")),
        check_vma=False,
    )
```

time: 147 us -> 65.9 us (0.45)
  Pallas kernels: 0 us -> 59.7 us
  local copies, waits for them, and re-layouts: 50.3 us -> 3.49 us
  waiting for transfers between devices: 36.5 us -> 0 us
  starting transfers between devices: 19.4 us -> 0 us
  matrix products: 18.2 us -> 0 us
  between operations: 15.3 us -> 1.37 us
  other arithmetic: 6.44 us -> 0 us
    pallas_call x0 -> x1, Pallas kernels: none -> 59.7 us  [per_device(): pl.pallas_call(functools.partial(kernel, tms, scs), out_shape=(jax.ShapeD...]
    all_to_all x4 -> x0, waiting for transfers between devices: 35 us -> none  [the longest x2 21.7 us: per_device(): lax.all_to_all(scaled, 'tm', split_axis=2, concat_axis=1, tiled=True)]
    all_to_all x4 -> x0, starting transfers between devices: 19.1 us -> none  [the longest x2 11.5 us: per_device(): lax.all_to_all(scaled, 'tm', split_axis=2, concat_axis=1, tiled=True)]
    dot_general x20 -> x0, matrix products: 18.2 us -> none  [the longest x12 13.8 us: network_term(): lax.dot_general(picked, link_blocks[link], (((2,), (1,)), ((0,), (0,))),...]
    unnamed x34 -> x12, local copies, waits for them, and re-layouts: 17.4 us -> 2.2 us
    gather x13 -> x0, local copies, waits for them, and re-layouts: 14.5 us -> none  [the longest x12 13.8 us: network_term(): picked = jnp.take(zone_major, zone_links[:, link], axis=0)]
    slice x11 -> x0, local copies, waits for them, and re-layouts: 4.85 us -> none  [the longest x10 4.6 us: temporal_term(): column = moved[scen, :, 0:bus_width]]
    all_to_all x2 -> x0, local copies, waits for them, and re-layouts: 3.68 us -> none  [per_device(): lax.all_to_all(scaled, 'tm', split_axis=2, concat_axis=1, tiled=True)]
  transfers between devices with their start and end apart: 6 -> 0, of which waited for: 5 -> 0; matrix products, arithmetic and copies ran while one was open for 38% -> 0% of each run, Pallas kernels for 0% -> 0%
where the time goes in v1:
time: 65.9 us; the launch traced here: 64.6 us
  Pallas kernels  59.7 us (91%)
  local copies, waits for them, and re-layouts  3.49 us (5%)
  between operations  1.37 us (2%)
    pallas_call x1, Pallas kernels, per_device(): pl.pallas_call(functools.partial(kernel, tms, scs), out_shape=(jax.ShapeD...  59.7 us
    unnamed x12, local copies, waits for them, and re-layouts  2.2 us

profile of v1, /device:TPU:0, one launch (start us, length us, event | category | flops | bytes accessed | tf_op | source)
XLA Modules:
  0.0 64.6 jit_solution(16694121780081671560)
XLA Ops:
  1.3 0.0 copy-start
  1.3 0.0 copy-start.1
  1.3 0.0 copy-start.2
  1.3 0.0 copy-start.3
  1.3 0.0 copy-start.4
  1.3 1.6 %copy.9.cot_ref = f32[4,42,1024]{2,1,0:T(8,128)S(1)} copy(f32[4,42,1024]{2,0,1:T(4,128)} %param.7) | data formatting | bytes 1376256 | tf_op args[0]
  2.9 0.0 copy-done
  2.9 0.0 copy-done.1
  2.9 0.0 copy-done.2
  2.9 0.0 copy-done.3
  2.9 0.0 copy-done.4
  3.0 59.7 %sweeps.1 = (f32[4,42,1024]{2,1,0:T(8,128)S(1)}, f32[42,128]{1,0:T(8,128)S(1)}) custom-call(f32[4,42,1024]{2,1,0:T(8,128)S(1)} %copy.9.cot_ref, bf16[4,192,128]{2,1,0:T(8,128)(2,1)S(1)} %bitcast.5, s32[8,6]{1,0:T(8,128)S(1)} %copy-done.2, f32[8,1,128]{2,1,0:T(1,128)S(1)} %bitcast.6, bf16[336,336]{1,0:T(8,128)(2,1)S(1)} %bitcast.4, s32[1]{0:T(128)S(6)} %copy.12.band_ref, ...), custom_call_target="tpu_custom_call" | custom-call | tf_op jit(solution)/shard_map/sweeps/pallas_call | solution.py:224
  62.7 1.3 %copy.10 = f32[4,42,1024]{2,0,1:T(4,128)} copy(f32[4,42,1024]{2,1,0:T(8,128)S(1)} %get-tuple-element.2) | data formatting | bytes 1376256 | tf_op jit(solution)/shard_map/sweeps/pallas_call | solution.py:224
  64.0 0.6 copy.13
Async XLA Ops:
  1.3 1.6 %copy-start = (bf16[1,336,336]{2,1,0:T(8,128)(2,1)S(1)}, bf16[1,336,336]{2,1,0:T(8,128)(2,1)}, u32[]{:S(2)}) copy-start(bf16[1,336,336]{2,1,0:T(8,128)(2,1)} %param.11) | copy-start | bytes 677380
  1.3 1.6 %copy-start.1 = (bf16[1,6,128,128]{3,2,1,0:T(8,128)(2,1)S(1)}, bf16[1,6,128,128]{3,2,1,0:T(8,128)(2,1)}, u32[]{:S(2)}) copy-start(bf16[1,6,128,128]{3,2,1,0:T(8,128)(2,1)} %param.8) | copy-start | bytes 589828
  1.3 1.6 %copy-start.2 = (s32[8,6]{1,0:T(8,128)S(1)}, s32[8,6]{1,0:T(8,128)}, u32[]{:S(2)}) copy-start(s32[8,6]{1,0:T(8,128)} %links_ref.1) | copy-start | bytes 580
  1.3 1.6 %copy-start.3 = (f32[1024]{0:T(1024)S(1)}, f32[1024]{0:T(1024)}, u32[]{:S(2)}) copy-start(f32[1024]{0:T(1024)} %param.10) | copy-start | bytes 12292
  1.3 1.6 %copy-start.4 = (s32[128]{0:T(128)S(1)}, s32[128]{0:T(128)}, u32[]{:S(2)}) copy-start(s32[128]{0:T(128)} %param.13) | copy-start | bytes 1540

commit v2 on v1

v2 whole, which is shorter than its diff:
```python
import functools

import jax
import jax.numpy as jnp
from jax import lax
from jax.experimental import pallas as pl
from jax.experimental.pallas import tpu as pltpu
from jax.sharding import PartitionSpec as P

SWEEPS = 2
MESH = pl.DeviceIdType.MESH
F32 = jnp.float32
BF16 = jnp.bfloat16


def kernel(
    tms, scs,
    cot_ref, blk_ref, links_ref, step_ref, coup_ref, band_ref, cand_ref,
    out_ref, sit_ref,
    adj, sbuf, recv, tsend, trecv, wall, pick, turned, gacc, gsum, grecv,
    s_send, s_recv, t_send, t_recv, wz_send, wz_recv, wx_send, wx_recv, wy_send, wy_recv,
    wc_send, wc_recv, g_send, g_recv,
):
    me = lax.axis_index("tm")
    mine = lax.axis_index("scen")
    hours, scens, _ = cot_ref.shape
    zones, rows, bus = adj.shape
    parts, width, depth = wall.shape[:3]
    fan = links_ref.shape[1]
    share = zones // scs
    used = hours * scens
    total = tms * hours
    padded = gsum.shape[1]
    col = lax.rem(me, width)
    plane = lax.div(me, width)
    far_first = sorted(range(1, tms), key=lambda o: abs(2 * o - tms))
    both_last = (((1,), (1,)), ((), ()))

    barrier = pltpu.get_barrier_semaphore()
    for o in range(1, tms):
        pl.semaphore_signal(barrier, inc=1, device_id={"tm": lax.rem(me + o, tms)}, device_id_type=MESH)
    for o in range(1, scs):
        pl.semaphore_signal(barrier, inc=1, device_id={"scen": lax.rem(mine + o, scs)}, device_id_type=MESH)

    def remote(src, dst, send, got, axis, peer):
        copy = pltpu.make_async_remote_copy(
            src_ref=src, dst_ref=dst, send_sem=send, recv_sem=got,
            device_id={axis: peer}, device_id_type=MESH,
        )
        copy.start()
        return copy

    def scale(sweep, z):
        weighted = adj[z] * step_ref[z]
        sbuf[sweep, z] = weighted.astype(BF16)
        gacc[z] = weighted if sweep == 0 else gacc[z] + weighted

    def send_scaled(sweep, o):
        to = lax.rem(me + o, tms)
        return remote(
            sbuf.at[sweep, to], recv.at[sweep, me], s_send.at[sweep, o], s_recv.at[sweep, o], "tm", to
        )

    def temporal(sweep):
        side = recv[sweep].reshape(tms * rows, bus)
        copies = {}
        for o in far_first:
            to = lax.rem(me + o, tms)
            tsend[sweep, to] = jnp.dot(turned[to], side, preferred_element_type=F32).astype(BF16)
            copies[o] = remote(
                tsend.at[sweep, to], trecv.at[sweep, me], t_send.at[sweep, o], t_recv.at[sweep, o], "tm", to
            )
        trecv[sweep, me] = jnp.dot(turned[me], side, preferred_element_type=F32).astype(BF16)
        return copies

    def network(sweep):
        def one(z, _):
            picked = jnp.concatenate([sbuf[sweep, links_ref[z, k]] for k in range(fan)], axis=1)
            weights = jnp.concatenate(
                [wall[p, lax.rem(z, width), lax.div(z, width)] for p in range(parts)], axis=0
            )
            adj[z] = adj[z] - jnp.dot(picked, weights, preferred_element_type=F32)
            return 0

        lax.fori_loop(0, zones, one, 0, unroll=2)

    for z in range(zones):
        adj[z, used // 16 * 16:rows, :] = jnp.zeros((rows - used // 16 * 16, bus), F32)
        adj[z, 0:used, :] = cot_ref[:, :, z * bus:(z + 1) * bus].reshape(used, bus)
        scale(0, z)
    wall[mine, col, plane] = blk_ref[mine]
    pl.semaphore_wait(barrier, tms - 1 + scs - 1)

    along_z = []
    for o in range(1, depth):
        to = lax.rem(plane + o, depth) * width + col
        piece = wall.at[mine, col, plane]
        along_z.append(remote(piece, piece, wz_send.at[o], wz_recv.at[o], "tm", to))
    scaled_out = {o: send_scaled(0, o) for o in far_first}
    recv[0, me] = sbuf[0, me]

    spread = lax.broadcasted_iota(jnp.int32, (total, total), 0) - lax.broadcasted_iota(jnp.int32, (total, total), 1)
    masked = jnp.where(jnp.abs(spread) <= band_ref[0], coup_ref[...].astype(F32), 0.0).astype(BF16)
    at_row = lax.broadcasted_iota(jnp.int32, (rows, total), 0)
    ahead = at_row - scens * lax.broadcasted_iota(jnp.int32, (rows, total), 1)
    for j in range(tms):
        over = ahead + j * used
        pick[j] = jnp.where((over >= 0) & (over < scens) & (at_row < used), 1.0, 0.0).astype(BF16)

    def turn(j, _):
        half = lax.dot_general(pick[j], masked, both_last, preferred_element_type=F32).astype(BF16)
        whole = lax.dot_general(
            half, pick[...].reshape(tms * rows, total), both_last, preferred_element_type=F32
        )
        one = lax.broadcasted_iota(jnp.int32, (rows, tms * rows), 0)
        two = lax.broadcasted_iota(jnp.int32, (rows, tms * rows), 1)
        same = jnp.bitwise_and(one - two, scens - 1) == 0
        turned[j] = jnp.where(same, whole, 0.0).astype(BF16)
        return 0

    lax.fori_loop(0, tms, turn, 0)

    core = lax.rem(mine, 2)
    along_y = {}

    def to_same_core(back):
        held = lax.rem(col + width - back, width)
        for o in range(1, scs // 2):
            piece = wall.at[mine, held]
            along_y[o, back] = remote(
                piece, piece, wy_send.at[o, back], wy_recv.at[o, back], "scen", lax.rem(mine + 2 * o, scs)
            )

    for copy in along_z:
        copy.wait_recv()
    along_x = []
    for o in range(1, width):
        piece = wall.at[mine, col]
        to = plane * width + lax.rem(col + o, width)
        along_x.append(remote(piece, piece, wx_send.at[o], wx_recv.at[o], "tm", to))
    to_same_core(0)
    for o in range(1, width):
        along_x[o - 1].wait_recv()
        to_same_core(o)

    for o in far_first:
        scaled_out[o].wait_recv()
    temporal_out = temporal(0)
    sent = along_z + along_x + list(along_y.values()) + list(scaled_out.values()) + list(temporal_out.values())

    to_core = []
    for o in range(scs // 2):
        if o > 0:
            for back in range(width):
                along_y[o, back].wait_recv()
        piece = wall.at[lax.rem(mine + scs - 2 * o, scs)]
        to_core.append(remote(piece, piece, wc_send.at[o], wc_recv.at[o], "scen", mine + 1 - 2 * core))
    for copy in to_core:
        copy.wait_recv()
    sent += to_core

    network(0)
    scaled_out = {}
    for o in far_first:
        zone = lax.rem(me + o, tms)
        temporal_out[tms - o].wait_recv()
        adj[zone] = adj[zone] - trecv[0, zone].astype(F32)
        scale(1, zone)
        scaled_out[o] = send_scaled(1, o)
    adj[me] = adj[me] - trecv[0, me].astype(F32)
    scale(1, me)
    recv[1, me] = sbuf[1, me]

    network(1)

    hour_of = lax.broadcasted_iota(jnp.int32, (padded, rows), 1) - scens * lax.broadcasted_iota(
        jnp.int32, (padded, rows), 0
    )
    fold = jnp.where((hour_of >= 0) & (hour_of < scens), 1.0 / (scens * scs), 0.0)

    def fold_zone(z, _):
        gsum[z] = jnp.dot(fold, gacc[z], preferred_element_type=F32, precision=lax.Precision.HIGHEST)
        return 0

    lax.fori_loop(0, zones, fold_zone, 0)
    grads = []
    for o in range(1, scs):
        peer = lax.rem(mine + o, scs)
        grads.append(remote(
            gsum.at[pl.ds(peer * share, share)], grecv.at[o], g_send.at[o], g_recv.at[o], "scen", peer
        ))

    for o in far_first:
        scaled_out[o].wait_recv()
    temporal_out = temporal(1)
    sent += list(scaled_out.values()) + list(temporal_out.values()) + grads

    for copy in grads:
        copy.wait_recv()
    summed = gsum[pl.ds(mine * share, share)]
    for o in range(1, scs):
        summed = summed + grecv[o]
    local = cand_ref[...] - mine * (share * bus)
    siting = jnp.zeros((padded, cand_ref.shape[1]), F32)
    for part in range(share):
        ids = lax.broadcasted_iota(jnp.int32, (bus, cand_ref.shape[1]), 0) + part * bus
        chosen = jnp.where(ids == local, 1.0, 0.0)
        siting = siting + jnp.dot(
            summed[part], chosen, preferred_element_type=F32, precision=lax.Precision.HIGHEST
        )
    sit_ref[...] = siting[0:hours]

    def finish(zone):
        value = adj[zone] - trecv[1, zone].astype(F32)
        lanes = pl.ds(pl.multiple_of(zone * bus, bus), bus)
        out_ref[:, :, lanes] = value[0:used].reshape(hours, scens, bus)

    finish(me)
    for o in far_first:
        temporal_out[tms - o].wait_recv()
        finish(lax.rem(me + o, tms))
    for copy in sent:
        copy.wait_send()


def per_device(tms, scs, cotangent, blocks, zone_links, step_size, coupling, ramp_band, candidates):
    scens, hours, buses = cotangent.shape
    _, fan, bus, _ = blocks.shape
    zones = buses // bus
    rows = -(-hours * scens // 16) * 16
    padded = -(-hours // 8) * 8
    cut = fan * bus // scs
    width = 1
    while 4 * width * width <= tms:
        width *= 2
    depth = tms // width
    vmem = pl.BlockSpec(memory_space=pltpu.VMEM)
    smem = pl.BlockSpec(memory_space=pltpu.SMEM)
    dma = pltpu.SemaphoreType.DMA
    adjoint, siting_gradient = pl.pallas_call(
        functools.partial(kernel, tms, scs),
        out_shape=(
            jax.ShapeDtypeStruct((hours, scens, buses), F32),
            jax.ShapeDtypeStruct((hours, candidates.shape[0]), F32),
        ),
        in_specs=[vmem, vmem, smem, vmem, vmem, smem, vmem],
        out_specs=(vmem, vmem),
        scratch_shapes=[
            pltpu.VMEM((zones, rows, bus), F32),
            pltpu.VMEM((SWEEPS, zones, rows, bus), BF16),
            pltpu.VMEM((SWEEPS, tms, rows, bus), BF16),
            pltpu.VMEM((SWEEPS, tms, rows, bus), BF16),
            pltpu.VMEM((SWEEPS, zones, rows, bus), BF16),
            pltpu.VMEM((scs, width, depth, cut, bus), BF16),
            pltpu.VMEM((tms, rows, tms * hours), BF16),
            pltpu.VMEM((tms, rows, tms * rows), BF16),
            pltpu.VMEM((zones, rows, bus), F32),
            pltpu.VMEM((zones, padded, bus), F32),
            pltpu.VMEM((scs, zones // scs, padded, bus), F32),
            dma((SWEEPS, tms)), dma((SWEEPS, tms)), dma((SWEEPS, tms)), dma((SWEEPS, tms)),
            dma((depth,)), dma((depth,)), dma((width,)), dma((width,)),
            dma((scs, width)), dma((scs, width)), dma((scs,)), dma((scs,)), dma((scs,)), dma((scs,)),
        ],
        compiler_params=pltpu.CompilerParams(
            collective_id=0, has_side_effects=True, vmem_limit_bytes=40 * 1024 * 1024
        ),
        name="sweeps",
    )(
        jnp.transpose(cotangent, (1, 0, 2)),
        blocks.reshape(scs, cut, bus),
        zone_links,
        step_size.reshape(zones, 1, bus),
        coupling.reshape(coupling.shape[1:]),
        ramp_band,
        candidates.reshape(1, -1),
    )
    return jnp.transpose(adjoint, (1, 0, 2)), siting_gradient


def solution(mesh):
    placed = (
        P("scen", "tm", None),
        P("tm", None, None, None),
        P(),
        P(),
        P("tm", None, None),
        P("tm"),
        P("scen"),
    )
    return jax.shard_map(
        functools.partial(per_device, mesh.shape["tm"], mesh.shape["scen"]),
        mesh=mesh,
        in_specs=placed,
        out_specs=(P("scen", "tm", None), P("tm", "scen")),
        check_vma=False,
    )
```

time: 65.9 us -> 53.4 us (0.81); the launches traced: 64.6 us -> 53 us
  Pallas kernels: 59.7 us -> 46.6 us
  local copies, waits for them, and re-layouts: 3.49 us -> 5.11 us
    pallas_call x1, Pallas kernels: 59.7 us -> 46.6 us  [per_device(): pl.pallas_call(functools.partial(kernel, tms, scs), out_shape=(jax.ShapeD...]
    unnamed x12 -> x14, local copies, waits for them, and re-layouts: 2.2 us -> 5.11 us
    pallas_call x1 -> x0, local copies, waits for them, and re-layouts: 1.29 us -> none  [per_device(): pl.pallas_call(functools.partial(kernel, tms, scs), out_shape=(jax.ShapeD...]
where the time goes in v2:
time: 53.4 us; the launch traced here: 53 us
  Pallas kernels  46.6 us (87%)
  local copies, waits for them, and re-layouts  5.11 us (10%)
  between operations  1.31 us (2%)
    pallas_call x1, Pallas kernels, per_device(): pl.pallas_call(functools.partial(kernel, tms, scs), out_shape=(jax.ShapeD...  46.6 us
    unnamed x14, local copies, waits for them, and re-layouts  5.11 us

profile of v2, /device:TPU:0, one launch (start us, length us, event | category | flops | bytes accessed | tf_op | source)
XLA Modules:
  0.0 53.0 jit_solution(2792877484895630077)
XLA Ops:
  1.3 0.0 copy-start.4
  1.3 0.0 copy-start.3
  1.3 0.0 copy-start.5
  1.3 0.7 %copy-done.4 = f32[1024]{0:T(1024)S(1)} copy-done((f32[1024]{0:T(1024)S(1)}, f32[1024]{0:T(1024)}, u32[]{:S(2)}) %copy-start.4) | copy-done | bytes 4120
  2.0 0.0 copy-done.3
  2.0 0.0 copy-done.5
  2.0 0.0 copy-start
  2.0 1.1 %copy-done = f32[4,42,1024]{2,0,1:T(4,128)S(1)} copy-done((f32[4,42,1024]{2,0,1:T(4,128)S(1)}, f32[4,42,1024]{2,0,1:T(4,128)}, u32[]{:S(2)}) %copy-start) | copy-done | bytes 688152
  3.1 0.0 copy-start.1
  3.1 0.9 %copy-done.1 = bf16[1,336,336]{2,1,0:T(8,128)(2,1)S(1)} copy-done((bf16[1,336,336]{2,1,0:T(8,128)(2,1)S(1)}, bf16[1,336,336]{2,1,0:T(8,128)(2,1)}, u32[]{:S(2)}) %copy-start.1) | copy-done | bytes 225816
  4.0 0.0 copy-start.2
  4.0 0.9 %copy-done.2 = bf16[1,6,128,128]{3,2,1,0:T(8,128)(2,1)S(1)} copy-done((bf16[1,6,128,128]{3,2,1,0:T(8,128)(2,1)S(1)}, bf16[1,6,128,128]{3,2,1,0:T(8,128)(2,1)}, u32[]{:S(2)}) %copy-start.2) | copy-done | bytes 196632
  5.0 46.6 %sweeps.1 = (f32[42,4,1024]{2,1,0:T(4,128)S(1)}, f32[42,128]{1,0:T(8,128)S(1)}) custom-call(f32[42,4,1024]{2,1,0:T(4,128)S(1)} %bitcast.7, bf16[4,192,128]{2,1,0:T(8,128)(2,1)S(1)} %bitcast.9, s32[8,6]{1,0:T(8,128)S(1)} %copy-done.3, f32[8,1,128]{2,1,0:T(1,128)S(1)} %bitcast.10, bf16[336,336]{1,0:T(8,128)(2,1)S(1)} %bitcast.8, s32[1]{0:T(128)S(6)} %copy.11.band_ref, ...), custom_call_target="tpu_custom_call" | custom-call | tf_op jit(solution)/shard_map/sweeps/pallas_call | solution.py:240
  51.5 0.8 %copy.12 = f32[4,42,1024]{2,0,1:T(4,128)} copy(f32[4,42,1024]{2,0,1:T(4,128)S(1)} %bitcast.6) | data formatting | bytes 1376256
  52.4 0.6 %copy.13 = f32[42,128]{1,0:T(8,128)} copy(f32[42,128]{1,0:T(8,128)S(1)} %get-tuple-element.9) | data formatting | bytes 43008
Async XLA Ops:
  1.3 0.7 %copy-start.4 = (f32[1024]{0:T(1024)S(1)}, f32[1024]{0:T(1024)}, u32[]{:S(2)}) copy-start(f32[1024]{0:T(1024)} %param.10) | copy-start | bytes 12292
  1.3 0.7 %copy-start.3 = (s32[8,6]{1,0:T(8,128)S(1)}, s32[8,6]{1,0:T(8,128)}, u32[]{:S(2)}) copy-start(s32[8,6]{1,0:T(8,128)} %links_ref.1) | copy-start | bytes 580
  1.3 0.7 %copy-start.5 = (s32[128]{0:T(128)S(1)}, s32[128]{0:T(128)}, u32[]{:S(2)}) copy-start(s32[128]{0:T(128)} %param.13) | copy-start | bytes 1540
  2.0 1.1 %copy-start = (f32[4,42,1024]{2,0,1:T(4,128)S(1)}, f32[4,42,1024]{2,0,1:T(4,128)}, u32[]{:S(2)}) copy-start(f32[4,42,1024]{2,0,1:T(4,128)} %param.7) | copy-start | bytes 2064388
  3.1 0.9 %copy-start.1 = (bf16[1,336,336]{2,1,0:T(8,128)(2,1)S(1)}, bf16[1,336,336]{2,1,0:T(8,128)(2,1)}, u32[]{:S(2)}) copy-start(bf16[1,336,336]{2,1,0:T(8,128)(2,1)} %param.11) | copy-start | bytes 677380
  4.0 0.9 %copy-start.2 = (bf16[1,6,128,128]{3,2,1,0:T(8,128)(2,1)S(1)}, bf16[1,6,128,128]{3,2,1,0:T(8,128)(2,1)}, u32[]{:S(2)}) copy-start(bf16[1,6,128,128]{3,2,1,0:T(8,128)(2,1)} %param.8) | copy-start | bytes 589828

commit v3 on v2

--- a/solution.py
+++ b/solution.py
@@ -15,8 +15,9 @@
 
 def kernel(
     tms, scs,
-    cot_ref, blk_ref, links_ref, step_ref, coup_ref, band_ref, cand_ref,
-    out_ref, sit_ref,
+    cot_hbm, blk_hbm, links_ref, step_hbm, coup_hbm, band_ref, cand_hbm,
+    out_hbm, sit_hbm,
+    cot_ref, step_ref, coup_ref, cand_ref, out_ref, sit_ref, in_sem, out_sem,
     adj, sbuf, recv, tsend, trecv, wall, pick, turned, gacc, gsum, grecv,
     s_send, s_recv, t_send, t_recv, wz_send, wz_recv, wx_send, wx_recv, wy_send, wy_recv,
     wc_send, wc_recv, g_send, g_recv,
@@ -36,6 +37,15 @@
     far_first = sorted(range(1, tms), key=lambda o: abs(2 * o - tms))
     both_last = (((1,), (1,)), ((), ()))
 
+    loads = [
+        pltpu.make_async_copy(src, dst, in_sem.at[i])
+        for i, (src, dst) in enumerate([
+            (cot_hbm, cot_ref), (step_hbm, step_ref), (blk_hbm.at[mine], wall.at[mine, col, plane]),
+            (coup_hbm, coup_ref), (cand_hbm, cand_ref),
+        ])
+    ]
+    for load in loads:
+        load.start()
     barrier = pltpu.get_barrier_semaphore()
     for o in range(1, tms):
         pl.semaphore_signal(barrier, inc=1, device_id={"tm": lax.rem(me + o, tms)}, device_id_type=MESH)
@@ -84,11 +94,13 @@
 
         lax.fori_loop(0, zones, one, 0, unroll=2)
 
+    loads[0].wait()
+    loads[1].wait()
     for z in range(zones):
         adj[z, used // 16 * 16:rows, :] = jnp.zeros((rows - used // 16 * 16, bus), F32)
         adj[z, 0:used, :] = cot_ref[:, :, z * bus:(z + 1) * bus].reshape(used, bus)
         scale(0, z)
-    wall[mine, col, plane] = blk_ref[mine]
+    loads[2].wait()
     pl.semaphore_wait(barrier, tms - 1 + scs - 1)
 
     along_z = []
@@ -99,6 +111,8 @@
     scaled_out = {o: send_scaled(0, o) for o in far_first}
     recv[0, me] = sbuf[0, me]
 
+    loads[3].wait()
+    loads[4].wait()
     spread = lax.broadcasted_iota(jnp.int32, (total, total), 0) - lax.broadcasted_iota(jnp.int32, (total, total), 1)
     masked = jnp.where(jnp.abs(spread) <= band_ref[0], coup_ref[...].astype(F32), 0.0).astype(BF16)
     at_row = lax.broadcasted_iota(jnp.int32, (rows, total), 0)
@@ -209,18 +223,25 @@
             summed[part], chosen, preferred_element_type=F32, precision=lax.Precision.HIGHEST
         )
     sit_ref[...] = siting[0:hours]
-
-    def finish(zone):
+    stores = [pltpu.make_async_copy(sit_ref, sit_hbm, out_sem.at[0])]
+    stores[0].start()
+
+    def finish(zone, o):
         value = adj[zone] - trecv[1, zone].astype(F32)
         lanes = pl.ds(pl.multiple_of(zone * bus, bus), bus)
         out_ref[:, :, lanes] = value[0:used].reshape(hours, scens, bus)
-
-    finish(me)
+        store = pltpu.make_async_copy(out_ref.at[:, :, lanes], out_hbm.at[:, :, lanes], out_sem.at[o + 1])
+        store.start()
+        stores.append(store)
+
+    finish(me, 0)
     for o in far_first:
         temporal_out[tms - o].wait_recv()
-        finish(lax.rem(me + o, tms))
+        finish(lax.rem(me + o, tms), o)
     for copy in sent:
         copy.wait_send()
+    for store in stores:
+        store.wait()
 
 
 def per_device(tms, scs, cotangent, blocks, zone_links, step_size, coupling, ramp_band, candidates):
@@ -234,7 +255,7 @@
     while 4 * width * width <= tms:
         width *= 2
     depth = tms // width
-    vmem = pl.BlockSpec(memory_space=pltpu.VMEM)
+    hbm = pl.BlockSpec(memory_space=pltpu.HBM)
     smem = pl.BlockSpec(memory_space=pltpu.SMEM)
     dma = pltpu.SemaphoreType.DMA
     adjoint, siting_gradient = pl.pallas_call(
@@ -243,9 +264,16 @@
             jax.ShapeDtypeStruct((hours, scens, buses), F32),
             jax.ShapeDtypeStruct((hours, candidates.shape[0]), F32),
         ),
-        in_specs=[vmem, vmem, smem, vmem, vmem, smem, vmem],
-        out_specs=(vmem, vmem),
+        in_specs=[hbm, hbm, smem, hbm, hbm, smem, hbm],
+        out_specs=(hbm, hbm),
         scratch_shapes=[
+            pltpu.VMEM((hours, scens, buses), F32),
+            pltpu.VMEM((zones, 1, bus), F32),
+            pltpu.VMEM(coupling.shape[1:], BF16),
+            pltpu.VMEM((1, candidates.shape[0]), jnp.int32),
+            pltpu.VMEM((hours, scens, buses), F32),
+            pltpu.VMEM((hours, candidates.shape[0]), F32),
+            dma((5,)), dma((tms + 1,)),
             pltpu.VMEM((zones, rows, bus), F32),
             pltpu.VMEM((SWEEPS, zones, rows, bus), BF16),
             pltpu.VMEM((SWEEPS, tms, rows, bus), BF16),
@@ -262,7 +290,7 @@
             dma((scs, width)), dma((scs, width)), dma((scs,)), dma((scs,)), dma((scs,)), dma((scs,)),
         ],
         compiler_params=pltpu.CompilerParams(
-            collective_id=0, has_side_effects=True, vmem_limit_bytes=40 * 1024 * 1024
+            collective_id=0, has_side_effects=True, vmem_limit_bytes=62 * 1024 * 1024
         ),
         name="sweeps",
     )(

time: 53.4 us -> 51.3 us (0.961)
  local copies, waits for them, and re-layouts: 5.11 us -> 2.61 us
    unnamed x14 -> x4, local copies, waits for them, and re-layouts: 5.11 us -> 2.61 us
where the time goes in v3:
time: 51.3 us; the launch traced here: 50.7 us
  Pallas kernels  46.8 us (91%)
  local copies, waits for them, and re-layouts  2.61 us (5%)
  between operations  1.29 us (3%)
    pallas_call x1, Pallas kernels, per_device(): pl.pallas_call(functools.partial(kernel, tms, scs), out_shape=(jax.ShapeD...  46.8 us
    unnamed x4, local copies, waits for them, and re-layouts  2.61 us

profile of v3, /device:TPU:0, one launch (start us, length us, event | category | flops | bytes accessed | tf_op | source)
XLA Modules:
  0.0 50.7 jit_solution(827396835419486866)
XLA Ops:
  1.3 46.8 %sweeps.1 = (f32[42,4,1024]{2,1,0:T(4,128)}, f32[42,128]{1,0:T(8,128)}) custom-call(f32[42,4,1024]{2,1,0:T(4,128)} %bitcast.7, bf16[4,192,128]{2,1,0:T(8,128)(2,1)} %bitcast.9, s32[8,6]{1,0:T(8,128)} %links_ref.1, f32[8,1,128]{2,1,0:T(1,128)} %bitcast.10, bf16[336,336]{1,0:T(8,128)(2,1)} %bitcast.8, s32[1]{0:T(128)S(6)} %copy.11.band_ref, s32[1,128]{1,0:T(1,128)} %bitcast.11), custom_call_target="tpu_custom_call" | custom-call | tf_op jit(solution)/shard_map/sweeps/pallas_call | solution.py:261
  48.1 0.0 copy-start
  48.1 2.0 %copy.12 = f32[4,42,1024]{2,0,1:T(4,128)} copy(f32[4,42,1024]{2,0,1:T(4,128)} %bitcast.6) | data formatting | bytes 1376256
  50.1 0.0 copy-done
  50.1 0.6 %copy.13 = f32[42,128]{1,0:T(8,128)} copy(f32[42,128]{1,0:T(8,128)S(1)} %copy-done) | data formatting | bytes 43008
Async XLA Ops:
  48.1 2.0 %copy-start = (f32[42,128]{1,0:T(8,128)S(1)}, f32[42,128]{1,0:T(8,128)}, u32[]{:S(2)}) copy-start(f32[42,128]{1,0:T(8,128)} %get-tuple-element.9) | copy-start | bytes 64516

commit v4 on v3

--- a/solution.py
+++ b/solution.py
@@ -60,6 +60,98 @@
         copy.start()
         return copy
 
+    core = lax.rem(mine, 2)
+    other = mine + 1 - 2 * core
+    pieces = [[(0, 0)]] + [[(hop, 0), (hop, 1)] for hop in range(1, depth)]
+
+    def held(back):
+        return lax.rem(col + width - back, width)
+
+    def on_piece(hop, way, action):
+        at = plane - hop * (1 - 2 * way)
+        if hop == 0:
+            action(at)
+        else:
+            pl.when((at >= 0) & (at < depth))(lambda: action(at))
+
+    def described(part, across, at, send, got, axis, peer):
+        place = wall.at[part, across, at]
+        return pltpu.make_async_remote_copy(
+            src_ref=place, dst_ref=place, send_sem=send, recv_sem=got,
+            device_id={axis: peer}, device_id_type=MESH,
+        )
+
+    def z_copy(hop, way, at):
+        to = (plane + 1 - 2 * way) * width + col
+        return described(mine, col, at, wz_send.at[way, hop], wz_recv.at[way, hop], "tm", to)
+
+    def x_copy(o, hop, way, at, across):
+        to = plane * width + lax.rem(col + o, width)
+        return described(mine, across, at, wx_send.at[o, way, hop], wx_recv.at[o, way, hop], "tm", to)
+
+    def y_copy(o, back, hop, way, at, part):
+        to = lax.rem(mine + 2 * o, scs)
+        return described(
+            part, held(back), at, wy_send.at[o, back, way, hop], wy_recv.at[o, back, way, hop], "scen", to
+        )
+
+    def core_copy(o, back, part):
+        place = wall.at[part, held(back)]
+        return pltpu.make_async_remote_copy(
+            src_ref=place, dst_ref=place, send_sem=wc_send.at[o, back], recv_sem=wc_recv.at[o, back],
+            device_id={"scen": other}, device_id_type=MESH,
+        )
+
+    def z_sends(hop, way, at, action):
+        for onward in (0, 1) if hop == 0 else (way,):
+            if hop + 1 < depth:
+                beyond = plane + 1 - 2 * onward
+                pl.when((beyond >= 0) & (beyond < depth))(
+                    lambda onward=onward: action(z_copy(hop + 1, onward, at))
+                )
+
+    def own_column(hop):
+        for way in (0, 1) if hop else (0,):
+            def arrived(at, way=way):
+                if hop:
+                    z_copy(hop, way, at).wait_recv()
+                z_sends(hop, way, at, lambda copy: copy.start())
+                for o in range(1, width):
+                    x_copy(o, hop, way, at, col).start()
+                for o in range(1, scs // 2):
+                    y_copy(o, 0, hop, way, at, mine).start()
+
+            on_piece(hop, way, arrived)
+
+    def other_columns(hop):
+        for way in (0, 1) if hop else (0,):
+            def arrived(at, way=way):
+                for back in range(1, width):
+                    x_copy(back, hop, way, at, held(back)).wait_recv()
+                    for o in range(1, scs // 2):
+                        y_copy(o, back, hop, way, at, mine).start()
+
+            on_piece(hop, way, arrived)
+
+    def from_chips(o, back):
+        for hop, way in sum(pieces, []):
+            on_piece(
+                hop, way,
+                lambda at: y_copy(o, back, hop, way, at, lax.rem(mine + scs - 2 * o, scs)).wait_recv(),
+            )
+
+    def all_sent():
+        for hop, way in sum(pieces, []):
+            def gone(at):
+                z_sends(hop, way, at, lambda copy: copy.wait_send())
+                for o in range(1, width):
+                    x_copy(o, hop, way, at, col).wait_send()
+                for back in range(width):
+                    for o in range(1, scs // 2):
+                        y_copy(o, back, hop, way, at, mine).wait_send()
+
+            on_piece(hop, way, gone)
+
     def scale(sweep, z):
         weighted = adj[z] * step_ref[z]
         sbuf[sweep, z] = weighted.astype(BF16)
@@ -103,11 +195,7 @@
     loads[2].wait()
     pl.semaphore_wait(barrier, tms - 1 + scs - 1)
 
-    along_z = []
-    for o in range(1, depth):
-        to = lax.rem(plane + o, depth) * width + col
-        piece = wall.at[mine, col, plane]
-        along_z.append(remote(piece, piece, wz_send.at[o], wz_recv.at[o], "tm", to))
+    own_column(0)
     scaled_out = {o: send_scaled(0, o) for o in far_first}
     recv[0, me] = sbuf[0, me]
 
@@ -132,43 +220,30 @@
         turned[j] = jnp.where(same, whole, 0.0).astype(BF16)
         return 0
 
-    lax.fori_loop(0, tms, turn, 0)
-
-    core = lax.rem(mine, 2)
-    along_y = {}
-
-    def to_same_core(back):
-        held = lax.rem(col + width - back, width)
-        for o in range(1, scs // 2):
-            piece = wall.at[mine, held]
-            along_y[o, back] = remote(
-                piece, piece, wy_send.at[o, back], wy_recv.at[o, back], "scen", lax.rem(mine + 2 * o, scs)
-            )
-
-    for copy in along_z:
-        copy.wait_recv()
-    along_x = []
-    for o in range(1, width):
-        piece = wall.at[mine, col]
-        to = plane * width + lax.rem(col + o, width)
-        along_x.append(remote(piece, piece, wx_send.at[o], wx_recv.at[o], "tm", to))
-    to_same_core(0)
-    for o in range(1, width):
-        along_x[o - 1].wait_recv()
-        to_same_core(o)
+    begin = 0
+    for hop in range(1, depth):
+        own_column(hop)
+        other_columns(hop - 1)
+        end = tms * hop // (depth - 1)
+        lax.fori_loop(begin, end, turn, 0)
+        begin = end
+    other_columns(depth - 1)
+    to_core = []
+    for back in range(width):
+        to_core.append(core_copy(0, back, mine))
+        to_core[-1].start()
+
 
     for o in far_first:
         scaled_out[o].wait_recv()
     temporal_out = temporal(0)
-    sent = along_z + along_x + list(along_y.values()) + list(scaled_out.values()) + list(temporal_out.values())
-
-    to_core = []
-    for o in range(scs // 2):
-        if o > 0:
-            for back in range(width):
-                along_y[o, back].wait_recv()
-        piece = wall.at[lax.rem(mine + scs - 2 * o, scs)]
-        to_core.append(remote(piece, piece, wc_send.at[o], wc_recv.at[o], "scen", mine + 1 - 2 * core))
+    sent = list(scaled_out.values()) + list(temporal_out.values())
+
+    for o in range(1, scs // 2):
+        for back in range(width):
+            from_chips(o, back)
+            to_core.append(core_copy(o, back, lax.rem(mine + scs - 2 * o, scs)))
+            to_core[-1].start()
     for copy in to_core:
         copy.wait_recv()
     sent += to_core
@@ -240,8 +315,23 @@
         finish(lax.rem(me + o, tms), o)
     for copy in sent:
         copy.wait_send()
+    all_sent()
     for store in stores:
         store.wait()
+
+
+def hand_on(adj_in, sit_in, adj_out, sit_out, sem):
+    hours = adj_in.shape[0]
+    cuts = 7 if hours % 7 == 0 else 1
+    step = hours // cuts
+    copies = [pltpu.make_async_copy(sit_in, sit_out, sem.at[cuts])]
+    for i in range(cuts):
+        rows = pl.ds(i * step, step)
+        copies.append(pltpu.make_async_copy(adj_in.at[rows], adj_out.at[rows], sem.at[i]))
+    for copy in copies:
+        copy.start()
+    for copy in copies:
+        copy.wait()
 
 
 def per_device(tms, scs, cotangent, blocks, zone_links, step_size, coupling, ramp_band, candidates):
@@ -286,8 +376,9 @@
             pltpu.VMEM((zones, padded, bus), F32),
             pltpu.VMEM((scs, zones // scs, padded, bus), F32),
             dma((SWEEPS, tms)), dma((SWEEPS, tms)), dma((SWEEPS, tms)), dma((SWEEPS, tms)),
-            dma((depth,)), dma((depth,)), dma((width,)), dma((width,)),
-            dma((scs, width)), dma((scs, width)), dma((scs,)), dma((scs,)), dma((scs,)), dma((scs,)),
+            dma((2, depth)), dma((2, depth)), dma((width, 2, depth)), dma((width, 2, depth)),
+            dma((scs, width, 2, depth)), dma((scs, width, 2, depth)), dma((scs, width)), dma((scs, width)),
+            dma((scs,)), dma((scs,)),
         ],
         compiler_params=pltpu.CompilerParams(
             collective_id=0, has_side_effects=True, vmem_limit_bytes=62 * 1024 * 1024
@@ -302,6 +393,18 @@
         ramp_band,
         candidates.reshape(1, -1),
     )
+    adjoint, siting_gradient = pl.pallas_call(
+        hand_on,
+        out_shape=(
+            jax.ShapeDtypeStruct(adjoint.shape, F32),
+            jax.ShapeDtypeStruct(siting_gradient.shape, F32),
+        ),
+        in_specs=[hbm, hbm],
+        out_specs=(hbm, hbm),
+        scratch_shapes=[dma((8,))],
+        compiler_params=pltpu.CompilerParams(vmem_limit_bytes=62 * 1024 * 1024),
+        name="hand_on",
+    )(adjoint, siting_gradient)
     return jnp.transpose(adjoint, (1, 0, 2)), siting_gradient
 
 

time: 51.3 us -> 74.8 us (1.46)
  Pallas kernels: 46.8 us -> 73.3 us
  local copies, waits for them, and re-layouts: 2.61 us -> 0 us
    pallas_call x0 -> x1, Pallas kernels: none -> 22.7 us  [per_device(): pl.pallas_call(hand_on, out_shape=(jax.ShapeDtypeStruct(adjoint.shape, F3...]
    pallas_call x1, Pallas kernels: 46.8 us -> 50.6 us  [per_device(): pl.pallas_call(functools.partial(kernel, tms, scs), out_shape=(jax.ShapeD...]
    unnamed x4 -> x0, local copies, waits for them, and re-layouts: 2.61 us -> none
where the time goes in v4:
time: 74.8 us; the launch traced here: 74.6 us
  Pallas kernels  73.3 us (98%)
  between operations  1.29 us (2%)
    pallas_call x1, Pallas kernels, per_device(): pl.pallas_call(functools.partial(kernel, tms, scs), out_shape=(jax.ShapeD...  50.6 us
    pallas_call x1, Pallas kernels, per_device(): pl.pallas_call(hand_on, out_shape=(jax.ShapeDtypeStruct(adjoint.shape, F3...  22.7 us

profile of v4, /device:TPU:0, one launch (start us, length us, event | category | flops | bytes accessed | tf_op | source)
XLA Modules:
  0.0 74.6 jit_solution(5391426654484037812)
XLA Ops:
  1.3 50.6 %sweeps.1 = (f32[42,4,1024]{2,1,0:T(4,128)}, f32[42,128]{1,0:T(8,128)}) custom-call(f32[42,4,1024]{2,1,0:T(4,128)} %bitcast.6, bf16[4,192,128]{2,1,0:T(8,128)(2,1)} %bitcast.8, s32[8,6]{1,0:T(8,128)} %links_ref.1, f32[8,1,128]{2,1,0:T(1,128)} %bitcast.9, bf16[336,336]{1,0:T(8,128)(2,1)} %bitcast.7, s32[1]{0:T(128)S(6)} %copy.9.band_ref, s32[1,128]{1,0:T(1,128)} %bitcast.10), custom_call_target="tpu_custom_call" | custom-call | tf_op jit(solution)/shard_map/sweeps/pallas_call | solution.py:351
  51.9 22.7 %hand_on.1 = (f32[42,4,1024]{2,1,0:T(4,128)}, f32[42,128]{1,0:T(8,128)}) custom-call(f32[42,4,1024]{2,1,0:T(4,128)} %get-tuple-element.6.adj_in, f32[42,128]{1,0:T(8,128)} %get-tuple-element.7.sit_in), custom_call_target="tpu_custom_call" | custom-call | tf_op jit(solution)/shard_map/hand_on/pallas_call | solution.py:396

commit v5 on v3

--- a/solution.py
+++ b/solution.py
@@ -18,7 +18,7 @@
     cot_hbm, blk_hbm, links_ref, step_hbm, coup_hbm, band_ref, cand_hbm,
     out_hbm, sit_hbm,
     cot_ref, step_ref, coup_ref, cand_ref, out_ref, sit_ref, in_sem, out_sem,
-    adj, sbuf, recv, tsend, trecv, wall, pick, turned, gacc, gsum, grecv,
+    adj, sbuf, recv, tsend, trecv, wall, turned, spread_in, spread_out, gacc, gsum, grecv,
     s_send, s_recv, t_send, t_recv, wz_send, wz_recv, wx_send, wx_recv, wy_send, wy_recv,
     wc_send, wc_recv, g_send, g_recv,
 ):
@@ -32,6 +32,7 @@
     used = hours * scens
     total = tms * hours
     padded = gsum.shape[1]
+    slot = rows // scens
     col = lax.rem(me, width)
     plane = lax.div(me, width)
     far_first = sorted(range(1, tms), key=lambda o: abs(2 * o - tms))
@@ -72,15 +73,21 @@
         )
 
     def temporal(sweep):
-        side = recv[sweep].reshape(tms * rows, bus)
+        spread_in[...] = recv[sweep].reshape(tms * rows, bus).astype(F32)
+        side = jnp.concatenate(
+            [spread_in[pl.ds(s, tms * slot, stride=scens), :].astype(BF16) for s in range(scens)], axis=1
+        )
+        term = jnp.dot(turned[...], side, preferred_element_type=F32)
+        for s in range(scens):
+            spread_out[pl.ds(s, tms * slot, stride=scens), :] = term[:, s * bus:(s + 1) * bus]
+        tsend[sweep] = spread_out[...].reshape(tms, rows, bus).astype(BF16)
         copies = {}
         for o in far_first:
             to = lax.rem(me + o, tms)
-            tsend[sweep, to] = jnp.dot(turned[to], side, preferred_element_type=F32).astype(BF16)
             copies[o] = remote(
                 tsend.at[sweep, to], trecv.at[sweep, me], t_send.at[sweep, o], t_recv.at[sweep, o], "tm", to
             )
-        trecv[sweep, me] = jnp.dot(turned[me], side, preferred_element_type=F32).astype(BF16)
+        trecv[sweep, me] = tsend[sweep, me]
         return copies
 
     def network(sweep):
@@ -115,24 +122,15 @@
     loads[4].wait()
     spread = lax.broadcasted_iota(jnp.int32, (total, total), 0) - lax.broadcasted_iota(jnp.int32, (total, total), 1)
     masked = jnp.where(jnp.abs(spread) <= band_ref[0], coup_ref[...].astype(F32), 0.0).astype(BF16)
-    at_row = lax.broadcasted_iota(jnp.int32, (rows, total), 0)
-    ahead = at_row - scens * lax.broadcasted_iota(jnp.int32, (rows, total), 1)
-    for j in range(tms):
-        over = ahead + j * used
-        pick[j] = jnp.where((over >= 0) & (over < scens) & (at_row < used), 1.0, 0.0).astype(BF16)
-
-    def turn(j, _):
-        half = lax.dot_general(pick[j], masked, both_last, preferred_element_type=F32).astype(BF16)
-        whole = lax.dot_general(
-            half, pick[...].reshape(tms * rows, total), both_last, preferred_element_type=F32
-        )
-        one = lax.broadcasted_iota(jnp.int32, (rows, tms * rows), 0)
-        two = lax.broadcasted_iota(jnp.int32, (rows, tms * rows), 1)
-        same = jnp.bitwise_and(one - two, scens - 1) == 0
-        turned[j] = jnp.where(same, whole, 0.0).astype(BF16)
-        return 0
-
-    lax.fori_loop(0, tms, turn, 0)
+    wide = lax.broadcasted_iota(jnp.int32, (tms * slot, 1), 0)
+    device = jnp.zeros_like(wide)
+    for j in range(1, tms):
+        device = device + (wide >= j * slot).astype(jnp.int32)
+    within = wide - device * slot
+    hour = jnp.where(within < hours, device * hours + within, -1)
+    pick = jnp.where(hour == lax.broadcasted_iota(jnp.int32, (tms * slot, total), 1), 1.0, 0.0).astype(BF16)
+    half = lax.dot_general(pick, masked, both_last, preferred_element_type=F32).astype(BF16)
+    turned[...] = lax.dot_general(half, pick, both_last, preferred_element_type=F32).astype(BF16)
 
     core = lax.rem(mine, 2)
     along_y = {}
@@ -242,6 +240,23 @@
         copy.wait_send()
     for store in stores:
         store.wait()
+
+
+def hand_on(adj_in, sit_in, adj_out, sit_out, adj, sit, sem):
+    hours = adj_in.shape[0]
+    cuts = 3 if hours % 3 == 0 else 1
+    step = hours // cuts
+    spans = [pl.ds(i * step, step) for i in range(cuts)]
+    legs = [(sit_in, sit, sit_out)] + [(adj_in.at[at], adj.at[at], adj_out.at[at]) for at in spans]
+    inward = [pltpu.make_async_copy(src, mid, sem.at[0, i]) for i, (src, mid, _) in enumerate(legs)]
+    outward = [pltpu.make_async_copy(mid, dst, sem.at[1, i]) for i, (_, mid, dst) in enumerate(legs)]
+    for copy in inward:
+        copy.start()
+    for first, second in zip(inward, outward):
+        first.wait()
+        second.start()
+    for copy in outward:
+        copy.wait()
 
 
 def per_device(tms, scs, cotangent, blocks, zone_links, step_size, coupling, ramp_band, candidates):
@@ -280,8 +295,9 @@
             pltpu.VMEM((SWEEPS, tms, rows, bus), BF16),
             pltpu.VMEM((SWEEPS, zones, rows, bus), BF16),
             pltpu.VMEM((scs, width, depth, cut, bus), BF16),
-            pltpu.VMEM((tms, rows, tms * hours), BF16),
-            pltpu.VMEM((tms, rows, tms * rows), BF16),
+            pltpu.VMEM((tms * (rows // scens), tms * (rows // scens)), BF16),
+            pltpu.VMEM((tms * rows, bus), F32),
+            pltpu.VMEM((tms * rows, bus), F32),
             pltpu.VMEM((zones, rows, bus), F32),
             pltpu.VMEM((zones, padded, bus), F32),
             pltpu.VMEM((scs, zones // scs, padded, bus), F32),
@@ -302,6 +318,20 @@
         ramp_band,
         candidates.reshape(1, -1),
     )
+    adjoint, siting_gradient = pl.pallas_call(
+        hand_on,
+        out_shape=(
+            jax.ShapeDtypeStruct(adjoint.shape, F32),
+            jax.ShapeDtypeStruct(siting_gradient.shape, F32),
+        ),
+        in_specs=[hbm, hbm],
+        out_specs=(hbm, hbm),
+        scratch_shapes=[
+            pltpu.VMEM(adjoint.shape, F32), pltpu.VMEM(siting_gradient.shape, F32), dma((2, 4)),
+        ],
+        compiler_params=pltpu.CompilerParams(vmem_limit_bytes=62 * 1024 * 1024),
+        name="hand_on",
+    )(adjoint, siting_gradient)
     return jnp.transpose(adjoint, (1, 0, 2)), siting_gradient
 
 

time: 51.3 us -> 51.2 us (level)
  Pallas kernels: 46.8 us -> 49.7 us
  local copies, waits for them, and re-layouts: 2.61 us -> 0 us
    unnamed x4 -> x0, local copies, waits for them, and re-layouts: 2.61 us -> none
    pallas_call x0 -> x1, Pallas kernels: none -> 1.93 us  [per_device(): pl.pallas_call(hand_on, out_shape=(jax.ShapeDtypeStruct(adjoint.shape, F3...]
    pallas_call x1, Pallas kernels: 46.8 us -> 47.8 us  [per_device(): pl.pallas_call(functools.partial(kernel, tms, scs), out_shape=(jax.ShapeD...]
where the time goes in v5:
time: 51.2 us; the launch traced here: 51 us
  Pallas kernels  49.7 us (97%)
  between operations  1.29 us (3%)
    pallas_call x1, Pallas kernels, per_device(): pl.pallas_call(functools.partial(kernel, tms, scs), out_shape=(jax.ShapeD...  47.8 us
    pallas_call x1, Pallas kernels, per_device(): pl.pallas_call(hand_on, out_shape=(jax.ShapeDtypeStruct(adjoint.shape, F3...  1.93 us

profile of v5, /device:TPU:0, one launch (start us, length us, event | category | flops | bytes accessed | tf_op | source)
XLA Modules:
  0.0 51.0 jit_solution(596272678276768073)
XLA Ops:
  1.3 47.8 %sweeps.1 = (f32[42,4,1024]{2,1,0:T(4,128)}, f32[42,128]{1,0:T(8,128)}) custom-call(f32[42,4,1024]{2,1,0:T(4,128)} %bitcast.6, bf16[4,192,128]{2,1,0:T(8,128)(2,1)} %bitcast.8, s32[8,6]{1,0:T(8,128)} %links_ref.1, f32[8,1,128]{2,1,0:T(1,128)} %bitcast.9, bf16[336,336]{1,0:T(8,128)(2,1)} %bitcast.7, s32[1]{0:T(128)S(6)} %copy.9.band_ref, s32[1,128]{1,0:T(1,128)} %bitcast.10), custom_call_target="tpu_custom_call" | custom-call | tf_op jit(solution)/shard_map/sweeps/pallas_call | solution.py:276
  49.1 1.9 %hand_on.1 = (f32[42,4,1024]{2,1,0:T(4,128)}, f32[42,128]{1,0:T(8,128)}) custom-call(f32[42,4,1024]{2,1,0:T(4,128)} %get-tuple-element.6.adj_in, f32[42,128]{1,0:T(8,128)} %get-tuple-element.7.sit_in), custom_call_target="tpu_custom_call" | custom-call | tf_op jit(solution)/shard_map/hand_on/pallas_call | solution.py:321

commit v6 on v4

--- a/solution.py
+++ b/solution.py
@@ -18,7 +18,7 @@
     cot_hbm, blk_hbm, links_ref, step_hbm, coup_hbm, band_ref, cand_hbm,
     out_hbm, sit_hbm,
     cot_ref, step_ref, coup_ref, cand_ref, out_ref, sit_ref, in_sem, out_sem,
-    adj, sbuf, recv, tsend, trecv, wall, pick, turned, gacc, gsum, grecv,
+    adj, sbuf, recv, tsend, trecv, wall, turned, spread_in, spread_out, gacc, gsum, grecv,
     s_send, s_recv, t_send, t_recv, wz_send, wz_recv, wx_send, wx_recv, wy_send, wy_recv,
     wc_send, wc_recv, g_send, g_recv,
 ):
@@ -32,6 +32,7 @@
     used = hours * scens
     total = tms * hours
     padded = gsum.shape[1]
+    slot = rows // scens
     col = lax.rem(me, width)
     plane = lax.div(me, width)
     far_first = sorted(range(1, tms), key=lambda o: abs(2 * o - tms))
@@ -164,15 +165,21 @@
         )
 
     def temporal(sweep):
-        side = recv[sweep].reshape(tms * rows, bus)
+        spread_in[...] = recv[sweep].reshape(tms * rows, bus).astype(F32)
+        side = jnp.concatenate(
+            [spread_in[pl.ds(s, tms * slot, stride=scens), :].astype(BF16) for s in range(scens)], axis=1
+        )
+        term = jnp.dot(turned[...], side, preferred_element_type=F32)
+        for s in range(scens):
+            spread_out[pl.ds(s, tms * slot, stride=scens), :] = term[:, s * bus:(s + 1) * bus]
+        tsend[sweep] = spread_out[...].reshape(tms, rows, bus).astype(BF16)
         copies = {}
         for o in far_first:
             to = lax.rem(me + o, tms)
-            tsend[sweep, to] = jnp.dot(turned[to], side, preferred_element_type=F32).astype(BF16)
             copies[o] = remote(
                 tsend.at[sweep, to], trecv.at[sweep, me], t_send.at[sweep, o], t_recv.at[sweep, o], "tm", to
             )
-        trecv[sweep, me] = jnp.dot(turned[me], side, preferred_element_type=F32).astype(BF16)
+        trecv[sweep, me] = tsend[sweep, me]
         return copies
 
     def network(sweep):
@@ -203,36 +210,24 @@
     loads[4].wait()
     spread = lax.broadcasted_iota(jnp.int32, (total, total), 0) - lax.broadcasted_iota(jnp.int32, (total, total), 1)
     masked = jnp.where(jnp.abs(spread) <= band_ref[0], coup_ref[...].astype(F32), 0.0).astype(BF16)
-    at_row = lax.broadcasted_iota(jnp.int32, (rows, total), 0)
-    ahead = at_row - scens * lax.broadcasted_iota(jnp.int32, (rows, total), 1)
-    for j in range(tms):
-        over = ahead + j * used
-        pick[j] = jnp.where((over >= 0) & (over < scens) & (at_row < used), 1.0, 0.0).astype(BF16)
-
-    def turn(j, _):
-        half = lax.dot_general(pick[j], masked, both_last, preferred_element_type=F32).astype(BF16)
-        whole = lax.dot_general(
-            half, pick[...].reshape(tms * rows, total), both_last, preferred_element_type=F32
-        )
-        one = lax.broadcasted_iota(jnp.int32, (rows, tms * rows), 0)
-        two = lax.broadcasted_iota(jnp.int32, (rows, tms * rows), 1)
-        same = jnp.bitwise_and(one - two, scens - 1) == 0
-        turned[j] = jnp.where(same, whole, 0.0).astype(BF16)
-        return 0
-
-    begin = 0
+    wide = lax.broadcasted_iota(jnp.int32, (tms * slot, 1), 0)
+    device = jnp.zeros_like(wide)
+    for j in range(1, tms):
+        device = device + (wide >= j * slot).astype(jnp.int32)
+    within = wide - device * slot
+    hour = jnp.where(within < hours, device * hours + within, -1)
+    pick = jnp.where(hour == lax.broadcasted_iota(jnp.int32, (tms * slot, total), 1), 1.0, 0.0).astype(BF16)
+    half = lax.dot_general(pick, masked, both_last, preferred_element_type=F32).astype(BF16)
+    turned[...] = lax.dot_general(half, pick, both_last, preferred_element_type=F32).astype(BF16)
+
     for hop in range(1, depth):
         own_column(hop)
         other_columns(hop - 1)
-        end = tms * hop // (depth - 1)
-        lax.fori_loop(begin, end, turn, 0)
-        begin = end
     other_columns(depth - 1)
     to_core = []
     for back in range(width):
         to_core.append(core_copy(0, back, mine))
         to_core[-1].start()
-
 
     for o in far_first:
         scaled_out[o].wait_recv()
@@ -320,17 +315,20 @@
         store.wait()
 
 
-def hand_on(adj_in, sit_in, adj_out, sit_out, sem):
+def hand_on(adj_in, sit_in, adj_out, sit_out, adj, sit, sem):
     hours = adj_in.shape[0]
-    cuts = 7 if hours % 7 == 0 else 1
+    cuts = 3 if hours % 3 == 0 else 1
     step = hours // cuts
-    copies = [pltpu.make_async_copy(sit_in, sit_out, sem.at[cuts])]
-    for i in range(cuts):
-        rows = pl.ds(i * step, step)
-        copies.append(pltpu.make_async_copy(adj_in.at[rows], adj_out.at[rows], sem.at[i]))
-    for copy in copies:
+    spans = [pl.ds(i * step, step) for i in range(cuts)]
+    legs = [(sit_in, sit, sit_out)] + [(adj_in.at[at], adj.at[at], adj_out.at[at]) for at in spans]
+    inward = [pltpu.make_async_copy(src, mid, sem.at[0, i]) for i, (src, mid, _) in enumerate(legs)]
+    outward = [pltpu.make_async_copy(mid, dst, sem.at[1, i]) for i, (_, mid, dst) in enumerate(legs)]
+    for copy in inward:
         copy.start()
-    for copy in copies:
+    for first, second in zip(inward, outward):
+        first.wait()
+        second.start()
+    for copy in outward:
         copy.wait()
 
 
@@ -370,8 +368,9 @@
             pltpu.VMEM((SWEEPS, tms, rows, bus), BF16),
             pltpu.VMEM((SWEEPS, zones, rows, bus), BF16),
             pltpu.VMEM((scs, width, depth, cut, bus), BF16),
-            pltpu.VMEM((tms, rows, tms * hours), BF16),
-            pltpu.VMEM((tms, rows, tms * rows), BF16),
+            pltpu.VMEM((tms * (rows // scens), tms * (rows // scens)), BF16),
+            pltpu.VMEM((tms * rows, bus), F32),
+            pltpu.VMEM((tms * rows, bus), F32),
             pltpu.VMEM((zones, rows, bus), F32),
             pltpu.VMEM((zones, padded, bus), F32),
             pltpu.VMEM((scs, zones // scs, padded, bus), F32),
@@ -401,7 +400,9 @@
         ),
         in_specs=[hbm, hbm],
         out_specs=(hbm, hbm),
-        scratch_shapes=[dma((8,))],
+        scratch_shapes=[
+            pltpu.VMEM(adjoint.shape, F32), pltpu.VMEM(siting_gradient.shape, F32), dma((2, 4)),
+        ],
         compiler_params=pltpu.CompilerParams(vmem_limit_bytes=62 * 1024 * 1024),
         name="hand_on",
     )(adjoint, siting_gradient)

time: 74.8 us -> 54.1 us (0.72)
  Pallas kernels: 73.3 us -> 52.6 us
    pallas_call x1, Pallas kernels: 22.7 us -> 1.93 us  [per_device(): pl.pallas_call(hand_on, out_shape=(jax.ShapeDtypeStruct(adjoint.shape, F3...]
where the time goes in v6:
time: 54.1 us; the launch traced here: 53.8 us
  Pallas kernels  52.6 us (97%)
  between operations  1.29 us (2%)
    pallas_call x1, Pallas kernels, per_device(): pl.pallas_call(functools.partial(kernel, tms, scs), out_shape=(jax.ShapeD...  50.6 us
    pallas_call x1, Pallas kernels, per_device(): pl.pallas_call(hand_on, out_shape=(jax.ShapeDtypeStruct(adjoint.shape, F3...  1.93 us

profile of v6, /device:TPU:0, one launch (start us, length us, event | category | flops | bytes accessed | tf_op | source)
XLA Modules:
  0.0 53.8 jit_solution(8947552658771624193)
XLA Ops:
  1.3 50.6 %sweeps.1 = (f32[42,4,1024]{2,1,0:T(4,128)}, f32[42,128]{1,0:T(8,128)}) custom-call(f32[42,4,1024]{2,1,0:T(4,128)} %bitcast.6, bf16[4,192,128]{2,1,0:T(8,128)(2,1)} %bitcast.8, s32[8,6]{1,0:T(8,128)} %links_ref.1, f32[8,1,128]{2,1,0:T(1,128)} %bitcast.9, bf16[336,336]{1,0:T(8,128)(2,1)} %bitcast.7, s32[1]{0:T(128)S(6)} %copy.9.band_ref, s32[1,128]{1,0:T(1,128)} %bitcast.10), custom_call_target="tpu_custom_call" | custom-call | tf_op jit(solution)/shard_map/sweeps/pallas_call | solution.py:349
  51.9 1.9 %hand_on.1 = (f32[42,4,1024]{2,1,0:T(4,128)}, f32[42,128]{1,0:T(8,128)}) custom-call(f32[42,4,1024]{2,1,0:T(4,128)} %get-tuple-element.6.adj_in, f32[42,128]{1,0:T(8,128)} %get-tuple-element.7.sit_in), custom_call_target="tpu_custom_call" | custom-call | tf_op jit(solution)/shard_map/hand_on/pallas_call | solution.py:395

commit v7 on v5

--- a/solution.py
+++ b/solution.py
@@ -35,7 +35,8 @@
     slot = rows // scens
     col = lax.rem(me, width)
     plane = lax.div(me, width)
-    far_first = sorted(range(1, tms), key=lambda o: abs(2 * o - tms))
+    by_reach = sorted(range(1, tms), key=lambda o: abs(2 * o - tms))
+    turns = [by_reach[i // 2] if i % 2 == 0 else by_reach[-1 - i // 2] for i in range(tms - 1)]
     both_last = (((1,), (1,)), ((), ()))
 
     loads = [
@@ -82,7 +83,7 @@
             spread_out[pl.ds(s, tms * slot, stride=scens), :] = term[:, s * bus:(s + 1) * bus]
         tsend[sweep] = spread_out[...].reshape(tms, rows, bus).astype(BF16)
         copies = {}
-        for o in far_first:
+        for o in turns:
             to = lax.rem(me + o, tms)
             copies[o] = remote(
                 tsend.at[sweep, to], trecv.at[sweep, me], t_send.at[sweep, o], t_recv.at[sweep, o], "tm", to
@@ -115,7 +116,7 @@
         to = lax.rem(plane + o, depth) * width + col
         piece = wall.at[mine, col, plane]
         along_z.append(remote(piece, piece, wz_send.at[o], wz_recv.at[o], "tm", to))
-    scaled_out = {o: send_scaled(0, o) for o in far_first}
+    scaled_out = {o: send_scaled(0, o) for o in turns}
     recv[0, me] = sbuf[0, me]
 
     loads[3].wait()
@@ -154,17 +155,17 @@
     for o in range(1, width):
         along_x[o - 1].wait_recv()
         to_same_core(o)
-
-    for o in far_first:
+    piece = wall.at[mine]
+    to_core = [remote(piece, piece, wc_send.at[0], wc_recv.at[0], "scen", mine + 1 - 2 * core)]
+
+    for o in turns:
         scaled_out[o].wait_recv()
     temporal_out = temporal(0)
     sent = along_z + along_x + list(along_y.values()) + list(scaled_out.values()) + list(temporal_out.values())
 
-    to_core = []
-    for o in range(scs // 2):
-        if o > 0:
-            for back in range(width):
-                along_y[o, back].wait_recv()
+    for o in range(1, scs // 2):
+        for back in range(width):
+            along_y[o, back].wait_recv()
         piece = wall.at[lax.rem(mine + scs - 2 * o, scs)]
         to_core.append(remote(piece, piece, wc_send.at[o], wc_recv.at[o], "scen", mine + 1 - 2 * core))
     for copy in to_core:
@@ -173,7 +174,7 @@
 
     network(0)
     scaled_out = {}
-    for o in far_first:
+    for o in [tms - o for o in turns]:
         zone = lax.rem(me + o, tms)
         temporal_out[tms - o].wait_recv()
         adj[zone] = adj[zone] - trecv[0, zone].astype(F32)
@@ -202,7 +203,7 @@
             gsum.at[pl.ds(peer * share, share)], grecv.at[o], g_send.at[o], g_recv.at[o], "scen", peer
         ))
 
-    for o in far_first:
+    for o in turns:
         scaled_out[o].wait_recv()
     temporal_out = temporal(1)
     sent += list(scaled_out.values()) + list(temporal_out.values()) + grads
@@ -233,7 +234,7 @@
         stores.append(store)
 
     finish(me, 0)
-    for o in far_first:
+    for o in [tms - o for o in turns]:
         temporal_out[tms - o].wait_recv()
         finish(lax.rem(me + o, tms), o)
     for copy in sent:

time: 51.2 us -> 51.8 us (1.012)
  Pallas kernels: 49.7 us -> 50.3 us
where the time goes in v7:
time: 51.8 us; the launch traced here: 51.5 us
  Pallas kernels  50.3 us (97%)
  between operations  1.29 us (2%)
    pallas_call x1, Pallas kernels, per_device(): pl.pallas_call(functools.partial(kernel, tms, scs), out_shape=(jax.ShapeD...  48.3 us
    pallas_call x1, Pallas kernels, per_device(): pl.pallas_call(hand_on, out_shape=(jax.ShapeDtypeStruct(adjoint.shape, F3...  1.93 us

profile of v7, /device:TPU:0, one launch (start us, length us, event | category | flops | bytes accessed | tf_op | source)
XLA Modules:
  0.0 51.5 jit_solution(14759337780748982913)
XLA Ops:
  1.3 48.3 %sweeps.1 = (f32[42,4,1024]{2,1,0:T(4,128)}, f32[42,128]{1,0:T(8,128)}) custom-call(f32[42,4,1024]{2,1,0:T(4,128)} %bitcast.6, bf16[4,192,128]{2,1,0:T(8,128)(2,1)} %bitcast.8, s32[8,6]{1,0:T(8,128)} %links_ref.1, f32[8,1,128]{2,1,0:T(1,128)} %bitcast.9, bf16[336,336]{1,0:T(8,128)(2,1)} %bitcast.7, s32[1]{0:T(128)S(6)} %copy.9.band_ref, s32[1,128]{1,0:T(1,128)} %bitcast.10), custom_call_target="tpu_custom_call" | custom-call | tf_op jit(solution)/shard_map/sweeps/pallas_call | solution.py:277
  49.6 1.9 %hand_on.1 = (f32[42,4,1024]{2,1,0:T(4,128)}, f32[42,128]{1,0:T(8,128)}) custom-call(f32[42,4,1024]{2,1,0:T(4,128)} %get-tuple-element.6.adj_in, f32[42,128]{1,0:T(8,128)} %get-tuple-element.7.sit_in), custom_call_target="tpu_custom_call" | custom-call | tf_op jit(solution)/shard_map/hand_on/pallas_call | solution.py:322

commit v8 on v5

--- a/solution.py
+++ b/solution.py
@@ -151,13 +151,13 @@
         to = plane * width + lax.rem(col + o, width)
         along_x.append(remote(piece, piece, wx_send.at[o], wx_recv.at[o], "tm", to))
     to_same_core(0)
+
+    for o in far_first:
+        scaled_out[o].wait_recv()
+    temporal_out = temporal(0)
     for o in range(1, width):
         along_x[o - 1].wait_recv()
         to_same_core(o)
-
-    for o in far_first:
-        scaled_out[o].wait_recv()
-    temporal_out = temporal(0)
     sent = along_z + along_x + list(along_y.values()) + list(scaled_out.values()) + list(temporal_out.values())
 
     to_core = []

time: 51.2 us -> 51.9 us (1.014)
  Pallas kernels: 49.7 us -> 50.4 us
    pallas_call x1, Pallas kernels: 47.8 us -> 48.5 us  [per_device(): pl.pallas_call(functools.partial(kernel, tms, scs), out_shape=(jax.ShapeD...]
where the time goes in v8:
time: 51.9 us; the launch traced here: 51.7 us
  Pallas kernels  50.4 us (97%)
  between operations  1.29 us (2%)
    pallas_call x1, Pallas kernels, per_device(): pl.pallas_call(functools.partial(kernel, tms, scs), out_shape=(jax.ShapeD...  48.5 us
    pallas_call x1, Pallas kernels, per_device(): pl.pallas_call(hand_on, out_shape=(jax.ShapeDtypeStruct(adjoint.shape, F3...  1.93 us

profile of v8, /device:TPU:0, one launch (start us, length us, event | category | flops | bytes accessed | tf_op | source)
XLA Modules:
  0.0 51.7 jit_solution(15592537956129653855)
XLA Ops:
  1.3 48.5 %sweeps.1 = (f32[42,4,1024]{2,1,0:T(4,128)}, f32[42,128]{1,0:T(8,128)}) custom-call(f32[42,4,1024]{2,1,0:T(4,128)} %bitcast.6, bf16[4,192,128]{2,1,0:T(8,128)(2,1)} %bitcast.8, s32[8,6]{1,0:T(8,128)} %links_ref.1, f32[8,1,128]{2,1,0:T(1,128)} %bitcast.9, bf16[336,336]{1,0:T(8,128)(2,1)} %bitcast.7, s32[1]{0:T(128)S(6)} %copy.9.band_ref, s32[1,128]{1,0:T(1,128)} %bitcast.10), custom_call_target="tpu_custom_call" | custom-call | tf_op jit(solution)/shard_map/sweeps/pallas_call | solution.py:276
  49.8 1.9 %hand_on.1 = (f32[42,4,1024]{2,1,0:T(4,128)}, f32[42,128]{1,0:T(8,128)}) custom-call(f32[42,4,1024]{2,1,0:T(4,128)} %get-tuple-element.6.adj_in, f32[42,128]{1,0:T(8,128)} %get-tuple-element.7.sit_in), custom_call_target="tpu_custom_call" | custom-call | tf_op jit(solution)/shard_map/hand_on/pallas_call | solution.py:321
